TPU v7x, 32 devices: a whole 2x2x4 slice. The times are simulated.
32 devices in a mesh: brick: 4 (over x, core), dom: 8 (over z, y).
Axes of the slice: x: 2, y: 2, z: 4, core: 2. Of those that a mesh axis runs over, the one named last changes fastest.
Arguments:
- velocity: bfloat16 [3, 27, 32768], P(None, None, ('brick', 'dom')), may hold values from -6 to 6
- adjoint: bfloat16 [3, 27, 32768], P(None, None, ('brick', 'dom')), may hold values from -6 to 6
- coupling: bfloat16 [27, 27], replicated, may hold values from -1.25 to 1.25
- jac_weight: float32 [32768], P(('brick', 'dom')), may hold values from 0.25 to 4
- owner: int32 [32768, 1], P(('brick', 'dom')), may hold values from 0 to 31; in each aligned block of 1024 rows (0 to 1023, 1024 to 2047, ...) at most 64 rows name the same one
- local_block: int32 [32768], P(('brick', 'dom')), may hold values from 0 to 4095
- offsets: int32 [128, 32768], P(None, ('brick', 'dom')), may hold values from 0 to 127
- margin: float32 [128, 32768], P(None, ('brick', 'dom')), may hold values from 0.002 to 0.02
- filtered: float32 [256, 512, 128], P('brick', 'dom'), may hold values from 0 to 1
Outputs:
- sensitivity: float32 [256, 512, 128], P('brick', 'dom')
- elem_density: float32 [32768], P(('brick', 'dom'))
Inputs may be any that keep to these rules, and one draw needn't show every extreme that they name: Among the 1024 elements of one device at most 64 have the same owner, and exactly 64 for some owner.
All inputs are finite; a program needn't handle non-finite values.
Results may differ from a plain program's by a relative error of at most 0.0003.
Values sent between devices are 32-bit elements; how exact they have to be, the bound alone decides.
No kernel may reach another device: no remote copies, remote signals or barrier semaphores. Data moves between devices by JAX's collectives and lax.ppermute only.
A program may use at most 64 MiB of HBM per device.

v0:
```python
import jax
import jax.numpy as jnp
from jax import lax
from jax.sharding import PartitionSpec as P

GZ = 128


sharpness = 8.0
threshold = 0.5
ramp_q = 0.1
radius_sq = 1.5
relax = 0.9


def padded(cells, sides, width):
    for axis, dim in sides:
        count = lax.axis_size(axis)
        ends = count - 1
        head = lax.slice_in_dim(cells, 0, width, axis=dim)
        tail = lax.slice_in_dim(cells, cells.shape[dim] - width, cells.shape[dim], axis=dim)
        cells = jnp.concatenate(
            [
                lax.ppermute(tail, axis, [(i, (i + 1) % count) for i in range(ends)]),
                cells,
                lax.ppermute(head, axis, [((i + 1) % count, i) for i in range(ends)]),
            ],
            axis=dim,
        )
    return cells


def project(field):
    base = jnp.tanh(sharpness * threshold)
    return (base + jnp.tanh(sharpness * (field - threshold))) / (
        base + jnp.tanh(sharpness * (1.0 - threshold))
    )


def projection_slope(field):
    base = jnp.tanh(sharpness * threshold)
    tangent = jnp.tanh(sharpness * (field - threshold))
    return sharpness * (1.0 - tangent * tangent) / (base + jnp.tanh(sharpness * (1.0 - threshold)))


def ramp_slope(density):
    return -ramp_q * (1.0 + ramp_q) / ((ramp_q + density) * (ramp_q + density))


def margin_rows(offsets, margin):
    entries, count = offsets.shape
    group = min(256, count)
    blocks = count // group
    lanes = jnp.arange(GZ, dtype=jnp.int32)
    grouped_offsets = offsets.reshape(entries, blocks, group).transpose(1, 0, 2)
    grouped_margin = margin.reshape(entries, blocks, group).transpose(1, 0, 2)

    def one_block(pair):
        block_offsets, block_margin = pair
        hits = block_offsets[:, :, None] == lanes[None, None, :]
        return jnp.sum(jnp.where(hits, block_margin[:, :, None], jnp.float32(0.0)), axis=0)

    return lax.map(one_block, (grouped_offsets, grouped_margin)).reshape(count, GZ)


def jacobi_extended(extended, source):
    padded_z = jnp.pad(extended, ((0, 0), (0, 0), (1, 1)))
    middle = extended[1:-1, 1:-1]
    near = extended[2:, 1:-1] + extended[:-2, 1:-1]
    near = near + extended[1:-1, 2:] + extended[1:-1, :-2]
    near = near + padded_z[1:-1, 1:-1, 2:] + padded_z[1:-1, 1:-1, :-2]
    center = 1.0 + 6.0 * radius_sq
    return middle + relax * (source - (center * middle - radius_sq * near)) / center


def body(velocity, adjoint, coupling, jac_weight, owner, local_block, offsets, margin, filtered):
    brick_count = lax.axis_size("brick")
    dom_count = lax.axis_size("dom")
    device_count = brick_count * dom_count
    element_count = owner.shape[0]
    width_x, width_y, depth = filtered.shape
    capacity = max(2, 2 * element_count // device_count)
    target = owner[:, 0]
    matches = (target[:, None] == jnp.arange(device_count, dtype=jnp.int32)[None, :]).astype(
        jnp.int32
    )
    position = jnp.sum(jnp.cumsum(matches, axis=0) * matches, axis=1) - 1
    placed = target * capacity + position
    voxel_rows = project(filtered).reshape(width_x * width_y, depth)
    weights = margin_rows(offsets, margin)
    mixed = jnp.einsum("ij,cje->cie", coupling, adjoint, preferred_element_type=jnp.float32)
    products = jac_weight * jnp.sum(velocity.astype(jnp.float32) * mixed, axis=(0, 1))
    requests = jnp.full((device_count * capacity,), -1, jnp.int32).at[placed].set(local_block)
    requests = requests.reshape(device_count, capacity)
    asked = lax.all_to_all(requests, ("brick", "dom"), split_axis=0, concat_axis=0, tiled=True)
    present = (asked >= 0).astype(jnp.float32)
    found = jnp.take(voxel_rows, jnp.maximum(asked, 0), axis=0) * present[..., None]
    returned = lax.all_to_all(found, ("brick", "dom"), split_axis=0, concat_axis=0, tiled=True)
    own_rows = returned.reshape(device_count * capacity, depth)[placed]
    density = jnp.sum(weights * own_rows, axis=1)
    terms = ramp_slope(density) * products
    outgoing = (
        jnp.zeros((device_count * capacity, depth), jnp.float32)
        .at[placed]
        .set(terms[:, None] * weights)
    )
    arrived = lax.all_to_all(
        outgoing.reshape(device_count, capacity, depth),
        ("brick", "dom"),
        split_axis=0,
        concat_axis=0,
        tiled=True,
    )
    arrived = arrived.reshape(device_count * capacity, depth)
    selector = (
        asked.reshape(1, -1) == jnp.arange(width_x * width_y, dtype=jnp.int32)[:, None]
    ).astype(jnp.float32)
    summed = jnp.dot(
        selector, arrived, precision=lax.Precision.HIGHEST, preferred_element_type=jnp.float32
    )
    source = summed.reshape(width_x, width_y, depth) * projection_slope(filtered)
    extended = padded(source, (("brick", 0), ("dom", 1)), 2)
    first = jacobi_extended(extended, extended[1:-1, 1:-1])
    place_x = lax.axis_index("brick") * width_x + jnp.arange(width_x + 2, dtype=jnp.int32) - 1
    place_y = lax.axis_index("dom") * width_y + jnp.arange(width_y + 2, dtype=jnp.int32) - 1
    inside_x = ((place_x >= 0) & (place_x < width_x * brick_count)).astype(jnp.float32)
    inside_y = ((place_y >= 0) & (place_y < width_y * dom_count)).astype(jnp.float32)
    first = first * (inside_x[:, None] * inside_y[None, :])[:, :, None]
    result = jacobi_extended(first, source)
    return (result, density)


def solution(mesh):
    return jax.shard_map(
        body,
        mesh=mesh,
        in_specs=(
            P(None, None, ("brick", "dom")),
            P(None, None, ("brick", "dom")),
            P(),
            P(("brick", "dom")),
            P(("brick", "dom"), None),
            P(("brick", "dom")),
            P(None, ("brick", "dom")),
            P(None, ("brick", "dom")),
            P("brick", "dom", None),
        ),
        out_specs=(P("brick", "dom", None), P(("brick", "dom"))),
        check_vma=False,
    )
```

profile of v0, /device:TPU:5, one launch (start us, length us, event | category | flops | bytes accessed | tf_op | source)
XLA Modules:
  0.0 176.3 jit_solution(6593738977648141309)
XLA Ops:
  0.6 0.7 fusion.31
  1.4 9.0 %reduce-window.6 = s32[32,8,128]{2,1,0:T(8,128)S(1)} reduce-window(s32[32,8,128]{2,1,0:T(8,128)S(1)} %fusion.31, s32[]{:T(128)} %constant.39.clone.1), window={size=1x1x128 pad=0_0x0_0x127_0}, to_apply=%region_0.0 | reduce-window | flops 4161536 | bytes 262148 | tf_op jit(solution)/shard_map/reduce-window
  10.4 0.1 slice.87
  10.5 0.1 copy.31
  10.7 0.1 copy.32
  10.8 0.1 broadcast_add_fusion
  10.9 0.7 fusion.30
  11.6 0.7 compare_select_fusion
  12.3 4.5 %scatter_custom_fusion = s32[2048]{0:T(1024)S(1)} fusion(s32[1024]{0:T(1024)S(1)} %bitcast.83, s32[1024]{0:T(1024)} %param.16, s32[]{:T(128)} %constant.35.clone.1), kind=kCustom, calls=%fused_computation.76 | custom fusion | bytes 8704 | tf_op jit(solution)/shard_map/scatter | solution.py:93
  16.8 0.7 all_to_all.12
  17.5 6.4 %all-to-all-start = ((s32[32,1,64]{2,1,0:T(1,128)}), s32[32,1,64]{2,1,0:T(1,128)S(1)}, u32[]{:S(2)}, u32[]{:S(2)}) async-start(s32[32,1,64]{2,1,0:T(1,128)} %all_to_all.12), calls=%async_computation | async-start | bytes 32768 | tf_op jit(solution)/shard_map/all_to_all | solution.py:95
  23.9 2.0 %add_multiply_fusion = f32[64,64,128]{2,1,0:T(8,128)S(1)} fusion(f32[64,64,128]{2,1,0:T(8,128)} %param.19), kind=kLoop, calls=%fused_computation.47 | loop fusion | flops 2097152 | bytes 4194304 | tf_op jit(solution)/shard_map/div | solution.py:35
  26.0 1.0 copy.33
  26.9 1.0 copy.34
  28.0 1.5 all-to-all-done
  29.5 0.1 reshape.172
  29.6 5.5 %gather_fusion = f32[2048,128]{1,0:T(8,128)S(1)} fusion(f32[4096,128]{1,0:T(8,128)S(1)} %bitcast.67, s32[2048]{0:T(1024)S(1)} %broadcast_clamp_fusion), kind=kCustom, calls=%fused_computation | custom fusion | bytes 2105344 | tf_op jit(solution)/shard_map/jit(_take)/gather | solution.py:97
  35.0 1.5 select_multiply_fusion
  36.5 4.3 %all-to-all-start.1 = ((f32[32,64,128]{2,1,0:T(8,128)}), f32[32,64,128]{2,1,0:T(8,128)S(1)}, u32[]{:S(2)}, u32[]{:S(2)}) async-start(f32[32,64,128]{2,1,0:T(8,128)} %select_multiply_fusion), calls=%async_computation.1 | async-start | bytes 2097152 | tf_op jit(solution)/shard_map/all_to_all | solution.py:98
  40.9 55.1 %while.11 = (s32[]{:T(128)}, f32[4,256,128]{2,1,0:T(8,128)}, s32[4,128,256]{1,2,0:T(8,128)}, f32[4,128,256]{1,2,0:T(8,128)}, s32[]{:T(128)}) while((s32[]{:T(128)}, f32[4,256,128]{2,1,0:T(8,128)}, s32[4,128,256]{1,2,0:T(8,128)}, f32[4,128,256]{1,2,0:T(8,128)}, s32[]{:T(128)}) %tuple.37), condition=%wide.region_6.7_spmd.clone, body=%wide.region_4.6_spmd.clone.sunk | while | flops 12550146 | bytes 1704017 | solution.py:63
  40.9 1.0 constant_dynamic-slice_fusion.4
  41.9 0.1 copy.46
  42.0 0.9 constant_dynamic-slice_fusion.5
  42.9 0.1 copy.47
  43.0 11.0 %select_reduce_fusion.2 = f32[256,128]{1,0:T(8,128)S(1)} fusion(f32[128,256]{1,0:T(8,128)S(1)} %bitcast.69, s32[128,256]{1,0:T(8,128)S(1)} %bitcast.70), kind=kLoop, calls=%fused_computation.6.clone.1 | loop fusion | flops 12550144 | bytes 393216 | tf_op jit(solution)/shard_map/while/body/eval_jaxpr/reduce_sum | solution.py:61
  54.1 0.7 bitcast_dynamic-update-slice_fusion.2
  54.7 0.9 constant_dynamic-slice_fusion.4
  55.6 0.1 copy.46
  55.7 0.9 constant_dynamic-slice_fusion.5
  56.7 0.1 copy.47
  56.8 11.0 %select_reduce_fusion.2 = f32[256,128]{1,0:T(8,128)S(1)} fusion(f32[128,256]{1,0:T(8,128)S(1)} %bitcast.69, s32[128,256]{1,0:T(8,128)S(1)} %bitcast.70), kind=kLoop, calls=%fused_computation.6.clone.1 | loop fusion | flops 12550144 | bytes 393216 | tf_op jit(solution)/shard_map/while/body/eval_jaxpr/reduce_sum | solution.py:61
  67.8 0.7 bitcast_dynamic-update-slice_fusion.2
  68.5 0.9 constant_dynamic-slice_fusion.4
  69.4 0.1 copy.46
  69.5 0.9 constant_dynamic-slice_fusion.5
  70.4 0.1 copy.47
  70.5 11.0 %select_reduce_fusion.2 = f32[256,128]{1,0:T(8,128)S(1)} fusion(f32[128,256]{1,0:T(8,128)S(1)} %bitcast.69, s32[128,256]{1,0:T(8,128)S(1)} %bitcast.70), kind=kLoop, calls=%fused_computation.6.clone.1 | loop fusion | flops 12550144 | bytes 393216 | tf_op jit(solution)/shard_map/while/body/eval_jaxpr/reduce_sum | solution.py:61
  81.6 0.7 bitcast_dynamic-update-slice_fusion.2
  82.2 0.9 constant_dynamic-slice_fusion.4
  83.1 0.1 copy.46
  83.2 0.9 constant_dynamic-slice_fusion.5
  84.2 0.1 copy.47
  84.3 11.0 %select_reduce_fusion.2 = f32[256,128]{1,0:T(8,128)S(1)} fusion(f32[128,256]{1,0:T(8,128)S(1)} %bitcast.69, s32[128,256]{1,0:T(8,128)S(1)} %bitcast.70), kind=kLoop, calls=%fused_computation.6.clone.1 | loop fusion | flops 12550144 | bytes 393216 | tf_op jit(solution)/shard_map/while/body/eval_jaxpr/reduce_sum | solution.py:61
  95.3 0.7 bitcast_dynamic-update-slice_fusion.2
  96.0 0.2 fusion.26
  96.3 2.8 %gather_fusion.1 = f32[1024,128]{1,0:T(8,128)S(1)} fusion(f32[2048,128]{1,0:T(8,128)S(1)} %bitcast.68, s32[1024]{0:T(1024)S(1)} %broadcast_clamp_fusion.1), kind=kCustom, calls=%fused_computation.1 | custom fusion | bytes 1052672 | tf_op jit(solution)/shard_map/gather | solution.py:99
  99.1 0.2 multiply_reduce_fusion
  99.4 0.2 bitcast_multiply_fusion
  99.6 4.1 %scatter_custom_fusion.1 = f32[2048,128]{1,0:T(8,128)} fusion(s32[1024]{0:T(1024)S(1)} %bitcast.85, f32[1024,128]{1,0:T(8,128)S(1)} %bitcast_multiply_fusion, f32[]{:T(128)} %constant.45.clone.1), kind=kCustom, calls=%fused_computation.55 | custom fusion | bytes 1048580 | tf_op jit(solution)/shard_map/scatter | solution.py:105
  103.6 5.8 %all-to-all-start.2 = ((f32[32,64,128]{2,1,0:T(8,128)}), f32[32,64,128]{2,1,0:T(8,128)S(1)}, u32[]{:S(2)}, u32[]{:S(2)}) async-start(f32[32,64,128]{2,1,0:T(8,128)} %bitcast.21), calls=%async_computation.2 | async-start | bytes 2097152 | tf_op jit(solution)/shard_map/all_to_all | solution.py:107
  109.5 0.6 broadcast.220
  110.1 0.7 reduce.4
  110.9 25.1 %all-to-all-done.2 = f32[32,64,128]{2,1,0:T(8,128)S(1)} async-done(((f32[32,64,128]{2,1,0:T(8,128)}), f32[32,64,128]{2,1,0:T(8,128)S(1)}, u32[]{:S(2)}, u32[]{:S(2)}) %all-to-all-start.2) | async-done | bytes 1048608 | tf_op jit(solution)/shard_map/all_to_all | solution.py:107
  136.0 16.5 %multiply_multiply_fusion = f32[64,64,128]{2,1,0:T(8,128)S(1)} fusion(f32[64,64,128]{2,1,0:T(8,128)S(1)} %copy-done.1, f32[2048,128,1]{1,0,2:T(8,128)S(1)} %bitcast.75, s32[64,64]{1,0:T(8,128)S(1)} %multiply_add_fusion, s32[2048]{0:T(1024)S(1)} %eq.74), kind=kOutput, calls=%fused_computation.46 | convolution fusion | flops 12896436224 | bytes 5267456 | tf_op jit(solution)/shard_map/dot_general | solution.py:118
  152.5 2.4 %collective-permute-start = (f32[2,64,128]{2,1,0:T(8,128)S(1)}, f32[2,64,128]{2,1,0:T(8,128)S(1)}, u32[]{:S(2)}, u32[]{:S(2)}) collective-permute-start(f32[2,64,128]{2,1,0:T(8,128)S(1)} %get-tuple-element.66), channel_id=1, source_target_pairs={{0,8},{8,16},{16,24},{1,9},{9,17},{17,25},{2,10},{10,18},{18,26},{... | collective-permute-start | bytes 196616 | tf_op jit(solution)/shard_map/ppermute | solution.py:24
  155.0 1.9 %collective-permute-start.1 = (f32[2,64,128]{2,1,0:T(8,128)S(1)}, f32[2,64,128]{2,1,0:T(8,128)S(1)}, u32[]{:S(2)}, u32[]{:S(2)}) collective-permute-start(f32[2,64,128]{2,1,0:T(8,128)S(1)} %get-tuple-element.67), channel_id=1, source_target_pairs={{8,0},{16,8},{24,16},{9,1},{17,9},{25,17},{10,2},{18,10},{26,18},{... | collective-permute-start | bytes 196616 | tf_op jit(solution)/shard_map/ppermute | solution.py:26
  156.9 3.6 %collective-permute-done.1 = f32[2,64,128]{2,1,0:T(8,128)S(1)} collective-permute-done((f32[2,64,128]{2,1,0:T(8,128)S(1)}, f32[2,64,128]{2,1,0:T(8,128)S(1)}, u32[]{:S(2)}, u32[]{:S(2)}) %collective-permute-start.1) | collective-permute-done | bytes 65568 | tf_op jit(solution)/shard_map/ppermute | solution.py:26
  160.6 2.5 %collective-permute-start.2 = (f32[68,2,128]{2,1,0:T(2,128)S(1)}, f32[68,2,128]{2,1,0:T(2,128)S(1)}, u32[]{:S(2)}, u32[]{:S(2)}) collective-permute-start(f32[68,2,128]{2,1,0:T(2,128)S(1)} %get-tuple-element.64), channel_id=1, source_target_pairs={{0,1},{1,2},{2,3},{3,4},{4,5},{5,6},{6,7},{8,9},{9,10},{10,11},{11... | collective-permute-start | bytes 208904 | tf_op jit(solution)/shard_map/ppermute | solution.py:24
  163.1 2.8 %collective-permute-start.3 = (f32[68,2,128]{2,1,0:T(2,128)S(1)}, f32[68,2,128]{2,1,0:T(2,128)S(1)}, u32[]{:S(2)}, u32[]{:S(2)}) collective-permute-start(f32[68,2,128]{2,1,0:T(2,128)S(1)} %get-tuple-element.65), channel_id=1, source_target_pairs={{1,0},{2,1},{3,2},{4,3},{5,4},{6,5},{7,6},{9,8},{10,9},{11,10},{12... | collective-permute-start | bytes 208904 | tf_op jit(solution)/shard_map/ppermute | solution.py:26
  165.9 0.1 broadcast_multiply_fusion
  166.0 3.1 %collective-permute-done.3 = f32[68,2,128]{2,1,0:T(2,128)S(1)} collective-permute-done((f32[68,2,128]{2,1,0:T(2,128)S(1)}, f32[68,2,128]{2,1,0:T(2,128)S(1)}, u32[]{:S(2)}, u32[]{:S(2)}) %collective-permute-start.3) | collective-permute-done | bytes 69664 | tf_op jit(solution)/shard_map/ppermute | solution.py:26
  169.1 0.4 pad_maximum_fusion
  169.5 3.9 %fusion.13 = f32[66,66,128]{2,1,0:T(8,128)S(1)} fusion(f32[68,68,128]{2,1,0:T(8,128)S(1)} %pad_maximum_fusion, f32[68,2,128]{2,1,0:T(2,128)S(1)} %collective-permute-done.2, f32[2,64,128]{2,1,0:T(8,128)S(1)} %collective-permute-done.1, f32[64,64,128]{2,1,0:T(8,128)S(1)} %multiply_multiply_fusion, f32[2,64,128]{2,1,0:T(8,128)S(1)} %collective-permute-done, ...), kind=kLoop, calls=%fused_computation.26 | loop fusion | flops 10036224 | bytes 14440448 | tf_op jit(solution)/shard_map/mul | solution.py:128
  173.4 2.9 %fusion.22 = f32[64,64,128]{2,1,0:T(8,128)} fusion(f32[64,64,128]{2,1,0:T(8,128)S(1)} %multiply_multiply_fusion, f32[66,66,128]{2,1,0:T(8,128)S(1)} %fusion.13), kind=kLoop, calls=%fused_computation.42 | loop fusion | flops 5767168 | bytes 17113088 | tf_op jit(solution)/shard_map/add | solution.py:73
  (36 shorter events, 0.3 us)
Async XLA Ops:
  0.6 95.4 %copy-start = (bf16[3,27,1024]{2,1,0:T(8,128)(2,1)S(1)}, bf16[3,27,1024]{2,1,0:T(8,128)(2,1)}, u32[]{:S(2)}) copy-start(bf16[3,27,1024]{2,1,0:T(8,128)(2,1)} %param.12) | copy-start | bytes 497668
  10.5 15.4 %copy-start.3 = (s32[128,1024]{1,0:T(8,128)S(1)}, s32[128,1024]{1,0:T(8,128)}, u32[]{:S(2)}) copy-start(s32[128,1024]{1,0:T(8,128)} %param.17) | copy-start | bytes 1572868
  17.5 12.0 %all-to-all-start = ((s32[32,1,64]{2,1,0:T(1,128)}), s32[32,1,64]{2,1,0:T(1,128)S(1)}, u32[]{:S(2)}, u32[]{:S(2)}) async-start(s32[32,1,64]{2,1,0:T(1,128)} %all_to_all.12), calls=%async_computation | async-start | bytes 32768 | tf_op jit(solution)/shard_map/all_to_all | solution.py:95
  23.9 3.1 %copy-start.4 = (f32[128,1024]{1,0:T(8,128)S(1)}, f32[128,1024]{1,0:T(8,128)}, u32[]{:S(2)}) copy-start(f32[128,1024]{1,0:T(8,128)} %param.18) | copy-start | bytes 1572868
  36.5 59.7 %all-to-all-start.1 = ((f32[32,64,128]{2,1,0:T(8,128)}), f32[32,64,128]{2,1,0:T(8,128)S(1)}, u32[]{:S(2)}, u32[]{:S(2)}) async-start(f32[32,64,128]{2,1,0:T(8,128)} %select_multiply_fusion), calls=%async_computation.1 | async-start | bytes 2097152 | tf_op jit(solution)/shard_map/all_to_all | solution.py:98
  40.9 55.1 %copy-start.7 = (bf16[3,27,1024]{2,1,0:T(8,128)(2,1)S(1)}, bf16[3,27,1024]{2,1,0:T(8,128)(2,1)}, u32[]{:S(2)}) copy-start(bf16[3,27,1024]{2,1,0:T(8,128)(2,1)} %param.11) | copy-start | bytes 497668
  40.9 55.1 %copy-start.8 = (bf16[27,27]{1,0:T(8,128)(2,1)S(1)}, bf16[27,27]{1,0:T(8,128)(2,1)}, u32[]{:S(2)}) copy-start(bf16[27,27]{1,0:T(8,128)(2,1)} %param.13) | copy-start | bytes 4378
  96.2 2.9 %copy-start.2 = (f32[4,256,128]{2,1,0:T(8,128)S(1)}, f32[4,256,128]{2,1,0:T(8,128)}, u32[]{:S(2)}) copy-start(f32[4,256,128]{2,1,0:T(8,128)} %get-tuple-element.29) | copy-start | bytes 1572868
  96.2 3.1 %copy-start.6 = (f32[1024]{0:T(1024)S(1)}, f32[1024]{0:T(1024)}, u32[]{:S(2)}) copy-start(f32[1024]{0:T(1024)} %param.14) | copy-start | bytes 12292
  99.1 36.9 %copy-start.1 = (f32[64,64,128]{2,1,0:T(8,128)S(1)}, f32[64,64,128]{2,1,0:T(8,128)}, u32[]{:S(2)}) copy-start(f32[64,64,128]{2,1,0:T(8,128)} %param.19) | copy-start | bytes 6291460
  99.3 53.2 %copy-start.5 = (f32[1,2,4,128]{3,1,2,0:T(2,128)}, f32[1,2,4,128]{3,1,2,0:T(2,128)S(1)}, u32[]{:S(2)}) copy-start(f32[1,2,4,128]{3,1,2,0:T(2,128)S(1)} %copy.42) | copy-start | bytes 12292
  103.6 32.3 %all-to-all-start.2 = ((f32[32,64,128]{2,1,0:T(8,128)}), f32[32,64,128]{2,1,0:T(8,128)S(1)}, u32[]{:S(2)}, u32[]{:S(2)}) async-start(f32[32,64,128]{2,1,0:T(8,128)} %bitcast.21), calls=%async_computation.2 | async-start | bytes 2097152 | tf_op jit(solution)/shard_map/all_to_all | solution.py:107
  152.5 4.4 %collective-permute-start = (f32[2,64,128]{2,1,0:T(8,128)S(1)}, f32[2,64,128]{2,1,0:T(8,128)S(1)}, u32[]{:S(2)}, u32[]{:S(2)}) collective-permute-start(f32[2,64,128]{2,1,0:T(8,128)S(1)} %get-tuple-element.66), channel_id=1, source_target_pairs={{0,8},{8,16},{16,24},{1,9},{9,17},{17,25},{2,10},{10,18},{18,26},{... | collective-permute-start | bytes 196616 | tf_op jit(solution)/shard_map/ppermute | solution.py:24
  155.0 5.6 %collective-permute-start.1 = (f32[2,64,128]{2,1,0:T(8,128)S(1)}, f32[2,64,128]{2,1,0:T(8,128)S(1)}, u32[]{:S(2)}, u32[]{:S(2)}) collective-permute-start(f32[2,64,128]{2,1,0:T(8,128)S(1)} %get-tuple-element.67), channel_id=1, source_target_pairs={{8,0},{16,8},{24,16},{9,1},{17,9},{25,17},{10,2},{18,10},{26,18},{... | collective-permute-start | bytes 196616 | tf_op jit(solution)/shard_map/ppermute | solution.py:26
  160.6 5.4 %collective-permute-start.2 = (f32[68,2,128]{2,1,0:T(2,128)S(1)}, f32[68,2,128]{2,1,0:T(2,128)S(1)}, u32[]{:S(2)}, u32[]{:S(2)}) collective-permute-start(f32[68,2,128]{2,1,0:T(2,128)S(1)} %get-tuple-element.64), channel_id=1, source_target_pairs={{0,1},{1,2},{2,3},{3,4},{4,5},{5,6},{6,7},{8,9},{9,10},{10,11},{11... | collective-permute-start | bytes 208904 | tf_op jit(solution)/shard_map/ppermute | solution.py:24
  163.1 6.0 %collective-permute-start.3 = (f32[68,2,128]{2,1,0:T(2,128)S(1)}, f32[68,2,128]{2,1,0:T(2,128)S(1)}, u32[]{:S(2)}, u32[]{:S(2)}) collective-permute-start(f32[68,2,128]{2,1,0:T(2,128)S(1)} %get-tuple-element.65), channel_id=1, source_target_pairs={{1,0},{2,1},{3,2},{4,3},{5,4},{6,5},{7,6},{9,8},{10,9},{11,10},{12... | collective-permute-start | bytes 208904 | tf_op jit(solution)/shard_map/ppermute | solution.py:26
where the time goes:
time: 178 us; the launch traced here: 176 us
  other arithmetic  67.6 us (38%)
  waiting for transfers between devices  33.3 us (19%)
  local copies, waits for them, and re-layouts  31.4 us (18%)
  starting transfers between devices  26.2 us (15%)
  matrix products  16.7 us (9%)
    reduce_sum x4, other arithmetic, one_block(): jnp.sum(jnp.where(hits, block_margin[:, :, None], jnp.float32(0.0)), axis=0)  44.2 us
    all_to_all x1, waiting for transfers between devices, body(): lax.all_to_all(outgoing.reshape(device_count, capacity, depth), ('brick',...  25.1 us
    dot_general x1, matrix products, body(): jnp.dot(selector, arrived, precision=lax.Precision.HIGHEST, preferred_ele...  16.5 us
    another operation x3, other arithmetic  9.15 us
    dynamic_slice x16, local copies, waits for them, and re-layouts, margin_rows(): lax.map(one_block, (grouped_offsets, grouped_margin)).reshape(count, GZ)  8.15 us
    ppermute x2, waiting for transfers between devices, padded(): lax.ppermute(head, axis, [((i + 1) % count, i) for i in range(ends)])  6.73 us
    all_to_all x1, starting transfers between devices, body(): lax.all_to_all(requests, ('brick', 'dom'), split_axis=0, concat_axis=0, t...  6.41 us
    all_to_all x1, starting transfers between devices, body(): lax.all_to_all(outgoing.reshape(device_count, capacity, depth), ('brick',...  5.84 us
  transfers between devices with their start and end apart: 7, of which 4 were waited for; matrix products, arithmetic and copies ran while one was open for 34% of the time, Pallas kernels for 0%

commit v1 on v0

v1 whole, which is shorter than its diff:
```python
import functools

import jax
import jax.numpy as jnp
from jax import lax
from jax.experimental import pallas as pl
from jax.experimental.pallas import tpu as pltpu
from jax.sharding import PartitionSpec as P

sharpness = 8.0
threshold = 0.5
ramp_q = 0.1
radius_sq = 1.5
relax = 0.9

VMEM_LIMIT = 48 * 1024 * 1024
BF16 = jnp.bfloat16
F32 = jnp.float32
I32 = jnp.int32


def params():
    return pltpu.CompilerParams(vmem_limit_bytes=VMEM_LIMIT)


def parts(x, count):
    found = []
    for _ in range(count - 1):
        head = x.astype(BF16)
        found.append(head)
        x = x - head.astype(F32)
    found.append(x.astype(BF16))
    return found


def dot_nt(a, b):
    return lax.dot_general(a, b, (((1,), (1,)), ((), ())), preferred_element_type=F32)


def dot_nn(a, b):
    return jnp.dot(a, b, preferred_element_type=F32)


def route_kernel(owner_ref, block_ref, jac_ref, vel_ref, adj_ref, coup_ref, meta_ref, rank_ref):
    devices, _, twice = meta_ref.shape
    capacity = twice // 2
    count = owner_ref.shape[1]
    group = 128
    owner = owner_ref[...]
    row_of = lax.broadcasted_iota(I32, (devices, group), 0)
    before = lax.broadcasted_iota(I32, (group, 2 * group), 0)
    after = lax.broadcasted_iota(I32, (group, 2 * group), 1)
    sums = ((before < after) | (after >= group)).astype(F32).astype(BF16)
    carry = jnp.zeros((devices, group), F32)
    matches, ranks = [], []
    for at in range(0, count, group):
        match = (row_of == owner[:, at : at + group]).astype(F32)
        totals = dot_nn(match.astype(BF16), sums)
        ranks.append(jnp.sum(match * (totals[:, :group] + carry), axis=0, keepdims=True))
        matches.append(match)
        carry = carry + totals[:, group:]
    rank = jnp.concatenate(ranks, axis=1).astype(I32)
    match = jnp.concatenate(matches, axis=1)
    rank_ref[...] = rank

    total = jnp.zeros((1, count), F32)
    for c in range(adj_ref.shape[0]):
        mixed = dot_nn(coup_ref[...], adj_ref[c])
        total = total + jnp.sum(vel_ref[c].astype(F32) * mixed, axis=0, keepdims=True)
    product = jac_ref[...] * total

    block = block_ref[...]
    pieces = [(block >> 6).astype(F32), (block & 63).astype(F32)]
    pieces += [p.astype(F32) for p in parts(product, 3)]
    at_rank = (lax.broadcasted_iota(I32, (capacity, count), 0) == rank).astype(F32).astype(BF16)
    left = jnp.concatenate([(match * p).astype(BF16) for p in pieces], axis=0)
    placed = dot_nt(left, at_rank)
    high, low, first, second, third = [
        placed[i * devices : (i + 1) * devices] for i in range(5)
    ]
    meta_ref[:, 0, :] = jnp.concatenate([high * 64.0 + low, first + (second + third)], axis=1)


def maps_kernel(rank_ref, owner_ref, off_ref, mar_ref, out_ref, map_ref):
    slots, depth = out_ref.shape
    entries, count = off_ref.shape
    group = 128
    sub = 8
    bands = depth // sub
    voxel = [lax.broadcasted_iota(I32, (sub, group), 0) + sub * k for k in range(bands)]

    for at in range(0, count, group):

        def step(chunk, totals, at=at):
            totals = list(totals)
            base = pl.multiple_of(chunk * sub, sub)
            offs = off_ref[pl.ds(base, sub), at : at + group]
            mars = mar_ref[pl.ds(base, sub), at : at + group]
            for s in range(sub):
                off = jnp.broadcast_to(offs[s : s + 1], (sub, group))
                mar = jnp.broadcast_to(mars[s : s + 1], (sub, group))
                for k in range(bands):
                    totals[k] = totals[k] + jnp.where(off == voxel[k], mar, 0.0)
            return tuple(totals)

        totals = lax.fori_loop(
            0, entries // sub, step, tuple(jnp.zeros((sub, group), F32) for _ in range(bands))
        )
        for k in range(bands):
            high, low = parts(totals[k], 2)
            map_ref[sub * k : sub * (k + 1), at : at + group] = high.astype(F32)
            map_ref[depth + sub * k : depth + sub * (k + 1), at : at + group] = low.astype(F32)


def place_kernel(capacity, rank_ref, owner_ref, off_ref, mar_ref, out_ref, map_ref):
    maps_kernel(rank_ref, owner_ref, off_ref, mar_ref, out_ref, map_ref)
    slots, depth = out_ref.shape
    count = off_ref.shape[1]
    place = owner_ref[...] * capacity + rank_ref[...]
    both = map_ref[...].astype(BF16)
    tile = 256
    for at in range(0, slots, tile):
        row_of = lax.broadcasted_iota(I32, (tile, count), 0) + at
        here = (row_of == place).astype(F32).astype(BF16)
        moved = dot_nt(here, both)
        out_ref[at : at + tile, :] = moved[:, :depth] + moved[:, depth:]


def gather_kernel(index_ref, field_ref, found_ref, slope_ref, proj_ref):
    rows = found_ref.shape[0]
    base = jnp.tanh(jnp.full((1, 1), sharpness * threshold, F32))
    ceiling = base + jnp.tanh(jnp.full((1, 1), sharpness * (1.0 - threshold), F32))
    tile = 256

    def project(i, _):
        at = pl.ds(pl.multiple_of(i * tile, tile), tile)
        tangent = jnp.tanh(sharpness * (field_ref[at, :] - threshold))
        proj_ref[at, :] = (base + tangent) / ceiling
        slope_ref[at, :] = sharpness * (1.0 - tangent * tangent) / ceiling
        return 0

    lax.fori_loop(0, field_ref.shape[0] // tile, project, 0)
    unroll = 16

    def fetch(i, _):
        for j in range(unroll):
            r = i * unroll + j
            found_ref[pl.ds(r, 1), :] = proj_ref[pl.ds(index_ref[r], 1), :]
        return 0

    lax.fori_loop(0, rows // unroll, fetch, 0)


def scatter_kernel(index_ref, prod_ref, weight_ref, found_ref, slope_ref, source_ref, ylow_ref, yhigh_ref, dens_ref, val_ref):
    rows, depth = weight_ref.shape
    width_x, width_y, _ = source_ref.shape
    ones = jnp.ones((2 * depth, depth), BF16)
    group = 128
    diagonal = lax.broadcasted_iota(I32, (group, depth), 0) == lax.broadcasted_iota(I32, (group, depth), 1)
    for at in range(0, rows, group):
        weight = weight_ref[at : at + group, :]
        high, low = parts(weight * found_ref[at : at + group, :], 2)
        density = dot_nn(jnp.concatenate([high, low], axis=1), ones)
        dens_ref[at // group : at // group + 1, :] = jnp.sum(
            jnp.where(diagonal, density, 0.0), axis=0, keepdims=True
        )
        shifted = ramp_q + density
        term = -ramp_q * (1.0 + ramp_q) / (shifted * shifted) * prod_ref[at : at + group, :]
        high, low = parts(term * weight, 2)
        val_ref[at : at + group, :depth] = high
        val_ref[at : at + group, depth:] = low
    planes = 4
    tile = planes * width_y

    def step(i, _):
        row_of = lax.broadcasted_iota(I32, (tile, rows), 0) + i * tile
        here = (row_of == index_ref[...]).astype(F32).astype(BF16)
        summed = dot_nn(here, val_ref[...])
        at = pl.ds(pl.multiple_of(i * tile, tile), tile)
        source = (summed[:, :depth] + summed[:, depth:]) * slope_ref[at, :]
        source_ref[pl.ds(i * planes, planes), :, :] = source.reshape(planes, width_y, depth)
        return 0

    lax.fori_loop(0, width_x // planes, step, 0)
    ylow_ref[0] = source_ref[:, 0, :]
    ylow_ref[1] = source_ref[:, 1, :]
    yhigh_ref[0] = source_ref[:, width_y - 2, :]
    yhigh_ref[1] = source_ref[:, width_y - 1, :]


def along_z(x):
    lane = lax.broadcasted_iota(I32, x.shape, x.ndim - 1)
    depth = x.shape[-1]
    up = jnp.where(lane == 0, 0.0, pltpu.roll(x, 1, x.ndim - 1))
    down = jnp.where(lane == depth - 1, 0.0, pltpu.roll(x, depth - 1, x.ndim - 1))
    return up + down


def along_y(x, low, high):
    row = lax.broadcasted_iota(I32, x.shape, 0)
    count = x.shape[0]
    up = jnp.where(row == 0, jnp.broadcast_to(low, x.shape), pltpu.roll(x, 1, 0))
    down = jnp.where(row == count - 1, jnp.broadcast_to(high, x.shape), pltpu.roll(x, count - 1, 0))
    return up + down


def sweep_kernel(inside_ref, source_ref, xlow_ref, xhigh_ref, ylow_ref, yhigh_ref, edge_low_ref, edge_high_ref, corner_low_ref, corner_high_ref, out_ref, near_ref, nlow_ref, nhigh_ref):
    width_x, width_y, depth = source_ref.shape
    center = 1.0 + 6.0 * radius_sq
    spread = relax * radius_sq / center
    scale = relax / center
    near_ref[0] = inside_ref[0] * (
        along_z(xlow_ref[1])
        + along_y(xlow_ref[1], corner_low_ref[0:1], corner_low_ref[1:2])
        + xlow_ref[0]
        + source_ref[0]
    )
    near_ref[width_x + 1] = inside_ref[1] * (
        along_z(xhigh_ref[0])
        + along_y(xhigh_ref[0], corner_high_ref[0:1], corner_high_ref[1:2])
        + xhigh_ref[1]
        + source_ref[width_x - 1]
    )
    nlow_ref[...] = inside_ref[2] * (
        along_z(ylow_ref[1])
        + along_y(ylow_ref[1], corner_low_ref[0:1], corner_high_ref[0:1])
        + ylow_ref[0]
        + edge_low_ref[...]
    )
    nhigh_ref[...] = inside_ref[3] * (
        along_z(yhigh_ref[0])
        + along_y(yhigh_ref[0], corner_low_ref[1:2], corner_high_ref[1:2])
        + yhigh_ref[1]
        + edge_high_ref[...]
    )

    def neighbours(x, here, below, above, low, high):
        return along_z(here) + along_y(here, low, high) + below + above

    def first(x, _):
        near_ref[x + 1] = neighbours(
            x,
            source_ref[x],
            source_ref[x - 1],
            source_ref[x + 1],
            ylow_ref[1, pl.ds(x, 1), :],
            yhigh_ref[0, pl.ds(x, 1), :],
        )
        return 0

    near_ref[1] = neighbours(
        0, source_ref[0], xlow_ref[1], source_ref[1], ylow_ref[1, 0:1, :], yhigh_ref[0, 0:1, :]
    )
    lax.fori_loop(1, width_x - 1, first, 0)
    near_ref[width_x] = neighbours(
        width_x - 1,
        source_ref[width_x - 1],
        source_ref[width_x - 2],
        xhigh_ref[0],
        ylow_ref[1, width_x - 1 : width_x, :],
        yhigh_ref[0, width_x - 1 : width_x, :],
    )
    own = 1.0 - relax
    first_own = own + scale

    def second(x, _):
        here = near_ref[x + 1]
        again = neighbours(
            x,
            here,
            near_ref[x],
            near_ref[x + 2],
            nlow_ref[pl.ds(x, 1), :],
            nhigh_ref[pl.ds(x, 1), :],
        )
        out_ref[x] = (
            (own * first_own + scale) * source_ref[x]
            + (own * spread + spread * first_own) * here
            + (spread * spread) * again
        )
        return 0

    lax.fori_loop(0, width_x, second, 0)


def reply_kernel(rank_ref, owner_ref, reply_ref, out_ref):
    devices, capacity = reply_ref.shape
    count = rank_ref.shape[1]
    at_rank = (lax.broadcasted_iota(I32, (capacity, count), 0) == rank_ref[...]).astype(F32).astype(BF16)
    total = jnp.zeros((devices, count), F32)
    for piece in parts(reply_ref[...], 3):
        total = total + dot_nn(piece, at_rank)
    match = lax.broadcasted_iota(I32, (devices, count), 0) == owner_ref[...]
    out_ref[...] = jnp.sum(jnp.where(match, total, 0.0), axis=0, keepdims=True)


def shift(x, axis, up):
    count = lax.axis_size(axis)
    pairs = [(i, i + 1) if up else (i + 1, i) for i in range(count - 1)]
    return lax.ppermute(x, axis, pairs)


def body(velocity, adjoint, coupling, jac_weight, owner, local_block, offsets, margin, filtered):
    both = ("brick", "dom")
    brick_count = lax.axis_size("brick")
    dom_count = lax.axis_size("dom")
    devices = brick_count * dom_count
    count = owner.shape[0]
    width_x, width_y, depth = filtered.shape
    capacity = max(2, 2 * count // devices)
    slots = devices * capacity
    shape = jax.ShapeDtypeStruct

    owner_row = owner.reshape(1, count)
    meta, rank = pl.pallas_call(
        route_kernel,
        out_shape=(shape((devices, 1, 2 * capacity), F32), shape((1, count), I32)),
        compiler_params=params(),
        name="route",
    )(
        owner_row,
        local_block.reshape(1, count),
        jac_weight.reshape(1, count),
        velocity,
        adjoint,
        coupling,
    )
    meta = lax.all_to_all(meta, both, split_axis=0, concat_axis=0, tiled=True)
    outgoing = pl.pallas_call(
        functools.partial(place_kernel, capacity),
        out_shape=shape((slots, depth), F32),
        scratch_shapes=[pltpu.VMEM((2 * depth, count), F32)],
        compiler_params=params(),
        name="maps",
    )(rank, owner_row, offsets, margin)
    weights = lax.all_to_all(
        outgoing.reshape(devices, capacity, depth), both, split_axis=0, concat_axis=0, tiled=True
    ).reshape(slots, depth)

    index = meta[:, 0, :capacity].reshape(slots).astype(I32)
    prods = jnp.broadcast_to(meta[:, 0, capacity:].reshape(slots, 1), (slots, depth))
    vmem = pl.BlockSpec(memory_space=pltpu.VMEM)
    smem = pl.BlockSpec(memory_space=pltpu.SMEM)
    found, slope = pl.pallas_call(
        gather_kernel,
        out_shape=(shape((slots, depth), F32), shape((width_x * width_y, depth), F32)),
        in_specs=[smem, vmem],
        out_specs=(vmem, vmem),
        scratch_shapes=[pltpu.VMEM((width_x * width_y, depth), F32)],
        compiler_params=params(),
        name="gather",
    )(index, filtered.reshape(width_x * width_y, depth))
    source, yfirst, ylast, density = pl.pallas_call(
        scatter_kernel,
        out_shape=(
            shape((width_x, width_y, depth), F32),
            shape((2, width_x, depth), F32),
            shape((2, width_x, depth), F32),
            shape((slots // 128, 128), F32),
        ),
        scratch_shapes=[pltpu.VMEM((slots, 2 * depth), BF16)],
        compiler_params=params(),
        name="scatter",
    )(index.reshape(1, slots), prods, weights, found, slope)

    reply = lax.all_to_all(
        density.reshape(devices, 1, capacity), both, split_axis=0, concat_axis=0, tiled=True
    )
    element_density = pl.pallas_call(
        reply_kernel,
        out_shape=shape((1, count), F32),
        compiler_params=params(),
        name="reply",
    )(rank, owner_row, reply.reshape(devices, capacity))

    ylow = shift(ylast, "dom", True)
    yhigh = shift(yfirst, "dom", False)
    top = jnp.concatenate(
        [source[width_x - 2], source[width_x - 1], ylow[1, width_x - 1 :], yhigh[0, width_x - 1 :], jnp.zeros((6, depth), F32)]
    )
    bottom = jnp.concatenate(
        [source[0], source[1], ylow[1, :1], yhigh[0, :1], jnp.zeros((6, depth), F32)]
    )
    from_low = shift(top, "brick", True)
    from_high = shift(bottom, "brick", False)
    brick, dom = lax.axis_index("brick"), lax.axis_index("dom")
    inside = jnp.stack([brick > 0, brick < brick_count - 1, dom > 0, dom < dom_count - 1]).astype(F32)
    result = pl.pallas_call(
        sweep_kernel,
        out_shape=shape((width_x, width_y, depth), F32),
        in_specs=[smem] + [vmem] * 9,
        out_specs=vmem,
        scratch_shapes=[
            pltpu.VMEM((width_x + 2, width_y, depth), F32),
            pltpu.VMEM((width_x, depth), F32),
            pltpu.VMEM((width_x, depth), F32),
        ],
        compiler_params=params(),
        name="sweep",
    )(
        inside,
        source,
        from_low[: 2 * width_y].reshape(2, width_y, depth),
        from_high[: 2 * width_y].reshape(2, width_y, depth),
        ylow,
        yhigh,
        yfirst[0],
        ylast[1],
        from_low[2 * width_y : 2 * width_y + 8],
        from_high[2 * width_y : 2 * width_y + 8],
    )
    return (result, element_density.reshape(count))


def solution(mesh):
    return jax.shard_map(
        body,
        mesh=mesh,
        in_specs=(
            P(None, None, ("brick", "dom")),
            P(None, None, ("brick", "dom")),
            P(),
            P(("brick", "dom")),
            P(("brick", "dom"), None),
            P(("brick", "dom")),
            P(None, ("brick", "dom")),
            P(None, ("brick", "dom")),
            P("brick", "dom", None),
        ),
        out_specs=(P("brick", "dom", None), P(("brick", "dom"))),
        check_vma=False,
    )
```

time: 178 us -> 102 us (0.57)
  the two profiles are of different devices: /device:TPU:5 before, /device:TPU:0 now
where the time goes in v1:
time: 102 us; the launch traced here: 101 us
  Pallas kernels  38.2 us (37%)
  starting transfers between devices  25.8 us (25%)
  waiting for transfers between devices  23.9 us (23%)
  local copies, waits for them, and re-layouts  12.2 us (12%)
    all_to_all x1, waiting for transfers between devices, body(): lax.all_to_all(outgoing.reshape(devices, capacity, depth), both, split_ax...  21.3 us
    pallas_call x1, Pallas kernels, body(): pl.pallas_call(sweep_kernel, out_shape=shape((width_x, width_y, depth), F...  13.4 us
    unnamed x28, local copies, waits for them, and re-layouts  10.9 us
    ppermute x4, starting transfers between devices, shift(): return lax.ppermute(x, axis, pairs)  10.2 us
    pallas_call x1, Pallas kernels, body(): pl.pallas_call(functools.partial(place_kernel, capacity), out_shape=shape...  9.75 us
    pallas_call x1, Pallas kernels, body(): pl.pallas_call(scatter_kernel, out_shape=(shape((width_x, width_y, depth)...  9.51 us
    all_to_all x1, starting transfers between devices, body(): meta = lax.all_to_all(meta, both, split_axis=0, concat_axis=0, tiled=True)  7.3 us
    all_to_all x1, starting transfers between devices, body(): lax.all_to_all(outgoing.reshape(devices, capacity, depth), both, split_ax...  5.83 us
  transfers between devices with their start and end apart: 7, of which 2 were waited for; matrix products, arithmetic and copies ran while one was open for 1% of the time, Pallas kernels for 14%

profile of v1, /device:TPU:0, one launch (start us, length us, event | category | flops | bytes accessed | tf_op | source)
XLA Modules:
  0.0 101.2 jit_solution(16648328858051992331)
XLA Ops:
  0.6 0.0 copy-start.6
  0.6 0.9 copy-done.6
  1.6 0.0 copy-start.7
  1.6 0.9 copy-done.7
  2.5 0.0 copy-start.8
  2.5 0.7 copy-done.8
  3.2 0.0 copy-start.11
  3.2 0.7 copy-done.11
  3.9 0.0 copy-start.12
  3.9 0.7 copy-done.12
  4.6 0.0 copy-start.13
  4.6 0.7 copy-done.13
  5.2 1.2 %route.1 = (f32[32,1,128]{2,1,0:T(1,128)}, s32[1,1024]{1,0:T(1,128)S(1)}) custom-call(s32[1,1024]{1,0:T(1,128)S(1)} %bitcast.41, s32[1,1024]{1,0:T(1,128)S(1)} %bitcast.44, f32[1,1024]{1,0:T(1,128)S(1)} %bitcast.45, bf16[3,27,1024]{2,1,0:T(8,128)(2,1)S(1)} %copy-done.6, bf16[3,27,1024]{2,1,0:T(8,128)(2,1)S(1)} %copy-done.7, bf16[27,27]{1,0:T(8,128)(2,1)S(1)} %copy-done.11), custom_call_target="tpu_custom_call" | custom-call | tf_op jit(solution)/shard_map/route/pallas_call | solution.py:315
  6.4 7.3 %all-to-all-start = ((f32[32,1,128]{2,1,0:T(1,128)}), f32[32,1,128]{2,1,0:T(1,128)S(1)}, u32[]{:S(2)}, u32[]{:S(2)}) async-start(f32[32,1,128]{2,1,0:T(1,128)} %get-tuple-element.10), calls=%async_computation | async-start | bytes 32768 | tf_op jit(solution)/shard_map/all_to_all | solution.py:328
  13.7 0.0 copy-start.4
  13.8 1.0 %copy-done.4 = s32[128,1024]{1,0:T(8,128)S(1)} copy-done((s32[128,1024]{1,0:T(8,128)S(1)}, s32[128,1024]{1,0:T(8,128)}, u32[]{:S(2)}) %copy-start.4) | copy-done | bytes 524312
  14.8 0.0 copy-start.5
  14.8 1.0 %copy-done.5 = f32[128,1024]{1,0:T(8,128)S(1)} copy-done((f32[128,1024]{1,0:T(8,128)S(1)}, f32[128,1024]{1,0:T(8,128)}, u32[]{:S(2)}) %copy-start.5) | copy-done | bytes 524312
  15.8 0.0 copy-start.9
  15.8 0.7 copy-done.9
  16.5 0.0 copy-start.1
  16.5 9.8 %maps.1 = f32[2048,128]{1,0:T(8,128)} custom-call(s32[1,1024]{1,0:T(1,128)S(1)} %get-tuple-element.11.rank_ref, s32[1,1024]{1,0:T(1,128)S(1)} %bitcast.42, s32[128,1024]{1,0:T(8,128)S(1)} %copy-done.4, f32[128,1024]{1,0:T(8,128)S(1)} %copy-done.5), custom_call_target="tpu_custom_call" | custom-call | tf_op jit(solution)/shard_map/maps/pallas_call | solution.py:329
  26.3 0.0 all-to-all-done
  26.3 5.8 %all-to-all-start.1 = ((f32[32,64,128]{2,1,0:T(8,128)}), f32[32,64,128]{2,1,0:T(8,128)S(1)}, u32[]{:S(2)}, u32[]{:S(2)}) async-start(f32[32,64,128]{2,1,0:T(8,128)} %bitcast.7), calls=%async_computation.1 | async-start | bytes 2097152 | tf_op jit(solution)/shard_map/all_to_all | solution.py:336
  32.1 0.1 add_convert_fusion.inside_ref
  32.2 0.1 slice_convert_fusion
  32.3 0.1 convert_element_type.13.index_ref
  32.4 0.1 broadcast_in_dim.7
  32.5 0.1 fusion
  32.5 0.1 convert_element_type.12.index_ref
  32.6 0.0 copy-done.1
  32.6 3.5 %gather.1 = (f32[2048,128]{1,0:T(8,128)S(1)}, f32[4096,128]{1,0:T(8,128)S(1)}) custom-call(s32[2048]{0:T(1024)S(1)} %convert_element_type.13.index_ref, f32[4096,128]{1,0:T(8,128)S(1)} %bitcast.37), custom_call_target="tpu_custom_call" | custom-call | tf_op jit(solution)/shard_map/gather/pallas_call | solution.py:344
  36.1 0.0 copy-start
  36.1 1.3 %copy-done = f32[4096,128]{1,0:T(8,128)} copy-done((f32[4096,128]{1,0:T(8,128)}, f32[4096,128]{1,0:T(8,128)S(1)}, u32[]{:S(2)}) %copy-start) | copy-done | bytes 2097176
  37.4 0.0 copy-start.2
  37.4 1.0 copy-done.2
  38.4 21.3 %all-to-all-done.1 = f32[32,64,128]{2,1,0:T(8,128)S(1)} async-done(((f32[32,64,128]{2,1,0:T(8,128)}), f32[32,64,128]{2,1,0:T(8,128)S(1)}, u32[]{:S(2)}, u32[]{:S(2)}) %all-to-all-start.1) | async-done | bytes 1048608 | tf_op jit(solution)/shard_map/all_to_all | solution.py:336
  59.7 0.3 broadcast_in_dim.8.prod_ref
  60.0 0.0 copy-start.3
  60.0 1.2 %copy-done.3 = f32[2048,128]{1,0:T(8,128)S(1)} copy-done((f32[2048,128]{1,0:T(8,128)S(1)}, f32[2048,128]{1,0:T(8,128)}, u32[]{:S(2)}) %copy-start.3) | copy-done | bytes 1048600
  61.3 0.0 copy-start.10
  61.3 9.5 %scatter.1 = (f32[64,64,128]{2,1,0:T(8,128)S(1)}, f32[2,64,128]{2,1,0:T(8,128)S(1)}, f32[2,64,128]{2,1,0:T(8,128)S(1)}, f32[16,128]{1,0:T(8,128)S(1)}) custom-call(s32[1,2048]{1,0:T(1,128)S(1)} %convert_element_type.12.index_ref, f32[2048,128]{1,0:T(8,128)S(1)} %broadcast_in_dim.8.prod_ref, f32[2048,128]{1,0:T(8,128)S(1)} %bitcast.36, ...), custom_call_target="tpu_custom_call" | custom-call | tf_op jit(solution)/shard_map/scatter/pallas_call | solution.py:353
  70.8 1.3 %collective-permute-start.1 = (f32[2,64,128]{2,1,0:T(8,128)S(1)}, f32[2,64,128]{2,1,0:T(8,128)S(1)}, u32[]{:S(2)}, u32[]{:S(2)}) collective-permute-start(f32[2,64,128]{2,1,0:T(8,128)S(1)} %get-tuple-element.16), channel_id=1, source_target_pairs={{1,0},{2,1},{3,2},{4,3},{5,4},{6,5},{7,6},{9,8},{10,9},{11,10},{12... | collective-permute-start | bytes 196616 | tf_op jit(solution)/shard_map/ppermute | solution.py:300
  72.1 4.5 %collective-permute-start = (f32[2,64,128]{2,1,0:T(8,128)S(1)}, f32[2,64,128]{2,1,0:T(8,128)S(1)}, u32[]{:S(2)}, u32[]{:S(2)}) collective-permute-start(f32[2,64,128]{2,1,0:T(8,128)S(1)} %get-tuple-element.15), channel_id=1, source_target_pairs={{0,1},{1,2},{2,3},{3,4},{4,5},{5,6},{6,7},{8,9},{9,10},{10,11},{11... | collective-permute-start | bytes 196616 | tf_op jit(solution)/shard_map/ppermute | solution.py:300
  76.7 0.7 reshape.59
  77.3 2.5 %all-to-all-start.2 = ((f32[32,1,64]{2,1,0:T(1,128)}), f32[32,1,64]{2,1,0:T(1,128)S(1)}, u32[]{:S(2)}, u32[]{:S(2)}) async-start(f32[32,1,64]{2,1,0:T(1,128)} %bitcast.22), calls=%async_computation.2 | async-start | bytes 32768 | tf_op jit(solution)/shard_map/all_to_all | solution.py:366
  79.9 0.0 collective-permute-done.1.yhigh_ref
  79.9 0.0 collective-permute-done.ylow_ref
  80.0 1.3 %collective-permute-start.3 = (f32[136,128]{1,0:T(8,128)S(1)}, f32[136,128]{1,0:T(8,128)S(1)}, u32[]{:S(2)}, u32[]{:S(2)}) collective-permute-start(f32[136,128]{1,0:T(8,128)S(1)} %concatenate.7), channel_id=1, source_target_pairs={{8,0},{16,8},{24,16},{9,1},{17,9},{25,17},{10,2},{18,10},{26,18},{... | collective-permute-start | bytes 208904 | tf_op jit(solution)/shard_map/ppermute | solution.py:300
  81.3 3.0 %collective-permute-start.2 = (f32[136,128]{1,0:T(8,128)S(1)}, f32[136,128]{1,0:T(8,128)S(1)}, u32[]{:S(2)}, u32[]{:S(2)}) collective-permute-start(f32[136,128]{1,0:T(8,128)S(1)} %concatenate.6), channel_id=1, source_target_pairs={{0,8},{8,16},{16,24},{1,9},{9,17},{17,25},{2,10},{10,18},{18,26},{... | collective-permute-start | bytes 208904 | tf_op jit(solution)/shard_map/ppermute | solution.py:300
  84.3 2.6 %all-to-all-done.2 = f32[32,1,64]{2,1,0:T(1,128)S(1)} async-done(((f32[32,1,64]{2,1,0:T(1,128)}), f32[32,1,64]{2,1,0:T(1,128)S(1)}, u32[]{:S(2)}, u32[]{:S(2)}) %all-to-all-start.2) | async-done | bytes 8224 | tf_op jit(solution)/shard_map/all_to_all | solution.py:366
  86.9 0.0 copy-done.10
  86.9 0.8 reply.1
  87.7 0.0 collective-permute-done.3
  87.8 0.0 collective-permute-done.2
  87.8 13.4 %sweep.1 = f32[64,64,128]{2,1,0:T(8,128)} custom-call(f32[4]{0:T(128)S(1)} %add_convert_fusion.inside_ref, f32[64,64,128]{2,1,0:T(8,128)S(1)} %get-tuple-element.14.source_ref, f32[2,64,128]{2,1,0:T(8,128)S(1)} %bitcast.39, f32[2,64,128]{2,1,0:T(8,128)S(1)} %bitcast.38, f32[2,64,128]{2,1,0:T(8,128)S(1)} %collective-permute-done.ylow_ref, ...), custom_call_target="tpu_custom_call" | custom-call | tf_op jit(solution)/shard_map/sweep/pallas_call | solution.py:388
  (11 shorter events, 0.1 us)
Async XLA Ops:
  0.6 0.9 copy-start.6
  1.6 0.9 copy-start.7
  2.5 0.7 copy-start.8
  3.2 0.7 copy-start.11
  3.9 0.7 copy-start.12
  4.6 0.7 copy-start.13
  6.4 19.8 %all-to-all-start = ((f32[32,1,128]{2,1,0:T(1,128)}), f32[32,1,128]{2,1,0:T(1,128)S(1)}, u32[]{:S(2)}, u32[]{:S(2)}) async-start(f32[32,1,128]{2,1,0:T(1,128)} %get-tuple-element.10), calls=%async_computation | async-start | bytes 32768 | tf_op jit(solution)/shard_map/all_to_all | solution.py:328
  13.7 1.0 %copy-start.4 = (s32[128,1024]{1,0:T(8,128)S(1)}, s32[128,1024]{1,0:T(8,128)}, u32[]{:S(2)}) copy-start(s32[128,1024]{1,0:T(8,128)} %off_ref.1) | copy-start | bytes 1572868
  14.8 1.0 %copy-start.5 = (f32[128,1024]{1,0:T(8,128)S(1)}, f32[128,1024]{1,0:T(8,128)}, u32[]{:S(2)}) copy-start(f32[128,1024]{1,0:T(8,128)} %mar_ref.1) | copy-start | bytes 1572868
  15.8 0.7 copy-start.9
  16.5 16.1 %copy-start.1 = (f32[64,64,128]{2,1,0:T(8,128)S(1)}, f32[64,64,128]{2,1,0:T(8,128)}, u32[]{:S(2)}) copy-start(f32[64,64,128]{2,1,0:T(8,128)} %param.17) | copy-start | bytes 6291460
  26.3 33.4 %all-to-all-start.1 = ((f32[32,64,128]{2,1,0:T(8,128)}), f32[32,64,128]{2,1,0:T(8,128)S(1)}, u32[]{:S(2)}, u32[]{:S(2)}) async-start(f32[32,64,128]{2,1,0:T(8,128)} %bitcast.7), calls=%async_computation.1 | async-start | bytes 2097152 | tf_op jit(solution)/shard_map/all_to_all | solution.py:336
  36.1 1.3 %copy-start = (f32[4096,128]{1,0:T(8,128)}, f32[4096,128]{1,0:T(8,128)S(1)}, u32[]{:S(2)}) copy-start(f32[4096,128]{1,0:T(8,128)S(1)} %get-tuple-element.13.slope_ref) | copy-start | bytes 6291460
  37.4 1.0 copy-start.2
  60.0 1.2 %copy-start.3 = (f32[2048,128]{1,0:T(8,128)S(1)}, f32[2048,128]{1,0:T(8,128)}, u32[]{:S(2)}) copy-start(f32[2048,128]{1,0:T(8,128)} %copy-done.2) | copy-start | bytes 3145732
  61.3 25.7 %copy-start.10 = (s32[1024,1]{0,1:T(1,128)S(1)}, s32[1024,1]{0,1:T(1,128)}, u32[]{:S(2)}) copy-start(s32[1024,1]{0,1:T(1,128)} %param.13) | copy-start | bytes 12292
  70.8 9.1 %collective-permute-start.1 = (f32[2,64,128]{2,1,0:T(8,128)S(1)}, f32[2,64,128]{2,1,0:T(8,128)S(1)}, u32[]{:S(2)}, u32[]{:S(2)}) collective-permute-start(f32[2,64,128]{2,1,0:T(8,128)S(1)} %get-tuple-element.16), channel_id=1, source_target_pairs={{1,0},{2,1},{3,2},{4,3},{5,4},{6,5},{7,6},{9,8},{10,9},{11,10},{12... | collective-permute-start | bytes 196616 | tf_op jit(solution)/shard_map/ppermute | solution.py:300
  72.1 7.8 %collective-permute-start = (f32[2,64,128]{2,1,0:T(8,128)S(1)}, f32[2,64,128]{2,1,0:T(8,128)S(1)}, u32[]{:S(2)}, u32[]{:S(2)}) collective-permute-start(f32[2,64,128]{2,1,0:T(8,128)S(1)} %get-tuple-element.15), channel_id=1, source_target_pairs={{0,1},{1,2},{2,3},{3,4},{4,5},{5,6},{6,7},{8,9},{9,10},{10,11},{11... | collective-permute-start | bytes 196616 | tf_op jit(solution)/shard_map/ppermute | solution.py:300
  77.3 9.6 %all-to-all-start.2 = ((f32[32,1,64]{2,1,0:T(1,128)}), f32[32,1,64]{2,1,0:T(1,128)S(1)}, u32[]{:S(2)}, u32[]{:S(2)}) async-start(f32[32,1,64]{2,1,0:T(1,128)} %bitcast.22), calls=%async_computation.2 | async-start | bytes 32768 | tf_op jit(solution)/shard_map/all_to_all | solution.py:366
  80.0 7.8 %collective-permute-start.3 = (f32[136,128]{1,0:T(8,128)S(1)}, f32[136,128]{1,0:T(8,128)S(1)}, u32[]{:S(2)}, u32[]{:S(2)}) collective-permute-start(f32[136,128]{1,0:T(8,128)S(1)} %concatenate.7), channel_id=1, source_target_pairs={{8,0},{16,8},{24,16},{9,1},{17,9},{25,17},{10,2},{18,10},{26,18},{... | collective-permute-start | bytes 208904 | tf_op jit(solution)/shard_map/ppermute | solution.py:300
  81.3 6.5 %collective-permute-start.2 = (f32[136,128]{1,0:T(8,128)S(1)}, f32[136,128]{1,0:T(8,128)S(1)}, u32[]{:S(2)}, u32[]{:S(2)}) collective-permute-start(f32[136,128]{1,0:T(8,128)S(1)} %concatenate.6), channel_id=1, source_target_pairs={{0,8},{8,16},{16,24},{1,9},{9,17},{17,25},{2,10},{10,18},{18,26},{... | collective-permute-start | bytes 208904 | tf_op jit(solution)/shard_map/ppermute | solution.py:300

commit v2 on v1

v2 whole, which is shorter than its diff:
```python
import functools

import jax
import jax.numpy as jnp
from jax import lax
from jax.experimental import pallas as pl
from jax.experimental.pallas import tpu as pltpu
from jax.sharding import PartitionSpec as P

sharpness = 8.0
threshold = 0.5
ramp_q = 0.1
radius_sq = 1.5
relax = 0.9

VMEM_LIMIT = 32 * 1024 * 1024
VMEM_WHOLE = 60 * 1024 * 1024
BF16 = jnp.bfloat16
F32 = jnp.float32
I32 = jnp.int32


def params(limit=VMEM_LIMIT):
    return pltpu.CompilerParams(vmem_limit_bytes=limit)


def parts(x, count):
    found = []
    for _ in range(count - 1):
        head = x.astype(BF16)
        found.append(head)
        x = x - head.astype(F32)
    found.append(x.astype(BF16))
    return found


def dot_nt(a, b):
    return lax.dot_general(a, b, (((1,), (1,)), ((), ())), preferred_element_type=F32)


def dot_nn(a, b):
    return jnp.dot(a, b, preferred_element_type=F32)


def fetch(sources, targets, sems):
    copies = [
        pltpu.make_async_copy(source, target, sems.at[i])
        for i, (source, target) in enumerate(zip(sources, targets))
    ]
    for copy in copies:
        copy.start()
    return copies


def send_kernel(owner_at, block_at, jac_at, vel_at, adj_at, coup_at, off_at, mar_at, out_ref, rank_ref, owner_ref, block_ref, jac_ref, vel_ref, adj_ref, coup_ref, off_ref, mar_ref, high_ref, low_ref, first_ref, second_ref, hist_ref, map_ref, sems, *, devices, capacity):
    copies = fetch(
        [off_at, mar_at, owner_at, block_at, jac_at, vel_at, adj_at, coup_at],
        [off_ref, mar_ref, owner_ref, block_ref, jac_ref, vel_ref, adj_ref, coup_ref],
        sems,
    )
    slots, depth = out_ref.shape
    stride = slots // devices
    entries, count = off_ref.shape
    group = 128

    row_of = lax.broadcasted_iota(I32, (devices, group), 0)
    before = lax.broadcasted_iota(I32, (group, 2 * group), 0)
    after = lax.broadcasted_iota(I32, (group, 2 * group), 1)
    sums = ((before < after) | (after >= group)).astype(F32).astype(BF16)
    for copy in copies[2:]:
        copy.wait()
    owner = owner_ref[...]
    carry = jnp.zeros((devices, group), F32)
    matches, ranks = [], []
    for at in range(0, count, group):
        match = (row_of == owner[:, at : at + group]).astype(F32)
        totals = dot_nn(match.astype(BF16), sums)
        ranks.append(jnp.sum(match * (totals[:, :group] + carry), axis=0, keepdims=True))
        matches.append(match)
        carry = carry + totals[:, group:]
    rank = jnp.concatenate(ranks, axis=1).astype(I32)
    match = jnp.concatenate(matches, axis=1)
    rank_ref[...] = rank

    total = jnp.zeros((1, count), F32)
    for c in range(adj_ref.shape[0]):
        mixed = dot_nn(coup_ref[...], adj_ref[c])
        total = total + jnp.sum(vel_ref[c].astype(F32) * mixed, axis=0, keepdims=True)
    product = jac_ref[...] * total

    block = block_ref[...]
    pieces = [(block >> 6).astype(F32), (block & 63).astype(F32)]
    pieces += [p.astype(F32) for p in parts(product, 3)]
    at_rank = (lax.broadcasted_iota(I32, (capacity, count), 0) == rank).astype(F32).astype(BF16)
    left = jnp.concatenate([(match * p).astype(BF16) for p in pieces], axis=0)
    placed = dot_nt(left, at_rank)
    high, low, first, second, third = [
        placed[i * devices : (i + 1) * devices] for i in range(5)
    ]
    meta = [high * 64.0 + low, first + (second + third)]
    if 2 * capacity < depth:
        meta.append(jnp.zeros((devices, depth - 2 * capacity), F32))
    meta = jnp.concatenate(meta, axis=1)

    sets = count // group
    lows = group // sets
    highs = depth // lows
    for copy in copies[:2]:
        copy.wait()
    for b in range(sets):
        off = off_ref[:, b * group : (b + 1) * group].T
        mar = mar_ref[:, b * group : (b + 1) * group].T
        first = mar.astype(BF16).astype(F32)
        high_ref[b] = off // lows
        low_ref[b] = off % lows
        first_ref[b] = first
        second_ref[b] = mar - first

    high_of = lax.broadcasted_iota(I32, (highs, entries), 0)
    low_of = lax.broadcasted_iota(I32, (lows, entries), 0)
    set_of = lax.broadcasted_iota(I32, (highs, group), 1) // lows
    unroll = 32

    def step(i, _):
        for j in range(unroll):
            g = i * unroll + j
            left, right = [], []
            for b in range(sets):
                here = jnp.broadcast_to(high_ref[b, pl.ds(g, 1), :], (highs, entries)) == high_of
                for part_ref in (first_ref, second_ref):
                    part = jnp.broadcast_to(part_ref[b, pl.ds(g, 1), :], (highs, entries))
                    left.append(jnp.where(here, part, 0.0))
                right.append(
                    (jnp.broadcast_to(low_ref[b, pl.ds(g, 1), :], (lows, entries)) == low_of).astype(F32)
                )
            both = dot_nt(
                jnp.concatenate(left, axis=0).astype(BF16),
                jnp.concatenate(right, axis=0).astype(BF16),
            )
            hist = jnp.zeros((highs, group), F32)
            for b in range(sets):
                at = 2 * highs * b
                total = both[at : at + highs] + both[at + highs : at + 2 * highs]
                hist = jnp.where(set_of == b, total, hist)
            hist_ref[pl.ds(pl.multiple_of(g * highs, highs), highs), :] = hist
        return 0

    lax.fori_loop(0, group // unroll, step, 0)
    for h in range(highs):
        turned = hist_ref[pl.ds(h, group, stride=highs), :].T
        first = turned.astype(BF16)
        second = (turned - first.astype(F32)).astype(BF16)
        for b in range(sets):
            columns = slice(b * group, (b + 1) * group)
            map_ref[h * lows : (h + 1) * lows, columns] = first[b * lows : (b + 1) * lows]
            map_ref[depth + h * lows : depth + (h + 1) * lows, columns] = second[b * lows : (b + 1) * lows]

    place = owner * stride + rank
    tile = slots // 4
    for at in range(0, slots, tile):
        row_of = lax.broadcasted_iota(I32, (tile, count), 0) + at
        here = (row_of == place).astype(F32).astype(BF16)
        moved = dot_nt(here, map_ref[...])
        out_ref[at : at + tile, :] = moved[:, :depth] + moved[:, depth:]
    for d in range(devices):
        row = d * stride + capacity
        out_ref[row : row + 1, :] = meta[d : d + 1, :]


def constants():
    base = jnp.tanh(jnp.full((1, 1), sharpness * threshold, F32))
    return base, base + jnp.tanh(jnp.full((1, 1), sharpness * (1.0 - threshold), F32))


def owner_kernel(got_ref, field_ref, source_ref, ylow_ref, yhigh_ref, dens_ref, meta_ref, block_ref, found_ref, val_ref, y_ref, number_ref, sem, *, capacity):
    devices = dens_ref.shape[0]
    stride = got_ref.shape[0] // devices
    depth = got_ref.shape[1]
    rows = devices * capacity
    width_x, width_y, _ = source_ref.shape
    group = 128

    for d in range(devices):
        row = d * stride + capacity
        meta_ref[d : d + 1, :] = got_ref[row : row + 1, :]
    meta = meta_ref[...]
    block_ref[...] = meta.astype(I32)
    copy = pltpu.make_async_copy(block_ref, number_ref, sem)
    copy.start()
    prods = meta.T
    joined = group // capacity
    index = [
        jnp.concatenate(
            [block_ref[d + j : d + j + 1, :capacity] for j in range(joined)], axis=1
        )
        for d in range(0, devices, joined)
    ]
    y_of = lax.broadcasted_iota(I32, (width_y, group), 0)
    for k, part in enumerate(index):
        y_ref[:, k * group : (k + 1) * group] = (y_of == part % width_y).astype(F32).astype(BF16)
    x_row = jnp.concatenate(index, axis=1) // width_y
    copy.wait()

    def look(d, _):
        for r in range(capacity):
            found_ref[pl.ds(d * capacity + r, 1), :] = field_ref[pl.ds(number_ref[d, r], 1), :]
        return 0

    lax.fori_loop(0, devices, look, 0)

    base, ceiling = constants()
    inverse = 1.0 / ceiling
    for d in range(devices):
        at = slice(d * capacity, (d + 1) * capacity)
        tangent = jnp.tanh(sharpness * (found_ref[at, :] - threshold))
        weight = got_ref[d * stride : d * stride + capacity, :]
        high, low = parts(weight * ((base + tangent) * inverse), 2)
        val_ref[at, :depth] = high
        val_ref[at, depth:] = low
    found_ref[...] = dot_nn(val_ref[...], jnp.ones((2 * depth, depth), BF16))
    diagonal = lax.broadcasted_iota(I32, (capacity, depth), 0) == lax.broadcasted_iota(I32, (capacity, depth), 1)
    for d in range(devices):
        at = slice(d * capacity, (d + 1) * capacity)
        density = found_ref[at, :]
        dens_ref[d, :, :] = jnp.sum(jnp.where(diagonal, density, 0.0), axis=0, keepdims=True)[:, :capacity]
        shifted = ramp_q + density
        term = -ramp_q * (1.0 + ramp_q) / (shifted * shifted) * prods[capacity : 2 * capacity, d : d + 1]
        high, low = parts(term * got_ref[d * stride : d * stride + capacity, :], 2)
        val_ref[at, :depth] = high
        val_ref[at, depth:] = low

    planes = 16
    tile = planes * width_y

    def step(i, _):
        here = []
        for j in range(planes):
            at_x = (x_row == i * planes + j).astype(F32)
            here.append(y_ref[...] * jnp.broadcast_to(at_x, (width_y, rows)).astype(BF16))
        summed = dot_nn(jnp.concatenate(here, axis=0), val_ref[...])
        at = pl.ds(pl.multiple_of(i * tile, tile), tile)
        tangent = jnp.tanh(sharpness * (field_ref[at, :] - threshold))
        slope = sharpness * inverse * (1.0 - tangent * tangent)
        source = (summed[:, :depth] + summed[:, depth:]) * slope
        source_ref[pl.ds(i * planes, planes), :, :] = source.reshape(planes, width_y, depth)
        return 0

    lax.fori_loop(0, width_x // planes, step, 0)
    ylow_ref[0] = source_ref[:, 0, :]
    ylow_ref[1] = source_ref[:, 1, :]
    yhigh_ref[0] = source_ref[:, width_y - 2, :]
    yhigh_ref[1] = source_ref[:, width_y - 1, :]


def along_z(x):
    lane = lax.broadcasted_iota(I32, x.shape, x.ndim - 1)
    depth = x.shape[-1]
    up = jnp.where(lane == 0, 0.0, pltpu.roll(x, 1, x.ndim - 1))
    down = jnp.where(lane == depth - 1, 0.0, pltpu.roll(x, depth - 1, x.ndim - 1))
    return up + down


def along_rows(x, low, high):
    row = lax.broadcasted_iota(I32, x.shape, 0)
    count = x.shape[0]
    up = jnp.where(row == 0, jnp.broadcast_to(low, x.shape), pltpu.roll(x, 1, 0))
    down = jnp.where(row == count - 1, jnp.broadcast_to(high, x.shape), pltpu.roll(x, count - 1, 0))
    return up + down


def sweep_kernel(inside_ref, source_ref, xlow_ref, xhigh_ref, ylow_ref, yhigh_ref, edge_low_ref, edge_high_ref, corner_low_ref, corner_high_ref, out_at, wide_ref, near_ref, out_ref, sems):
    width_x, width_y, depth = source_ref.shape
    pad = 8
    inner = slice(pad, pad + width_y)
    center = 1.0 + 6.0 * radius_sq
    spread = relax * radius_sq / center
    scale = relax / center
    own = 1.0 - relax
    first_own = own + scale
    planes = 8

    def widen(i, _):
        at = i * planes
        wide_ref[pl.ds(at + 2, planes), inner, :] = source_ref[pl.ds(at, planes)]
        return 0

    lax.fori_loop(0, width_x // planes, widen, 0)
    wide_ref[0:2, inner, :] = xlow_ref[...]
    wide_ref[width_x + 2 : width_x + 4, inner, :] = xhigh_ref[...]
    wide_ref[2 : width_x + 2, pad - 1, :] = ylow_ref[1]
    wide_ref[2 : width_x + 2, pad + width_y, :] = yhigh_ref[0]
    wide_ref[1, pad - 1 : pad, :] = corner_low_ref[0:1]
    wide_ref[1, pad + width_y : pad + width_y + 1, :] = corner_low_ref[1:2]
    wide_ref[width_x + 2, pad - 1 : pad, :] = corner_high_ref[0:1]
    wide_ref[width_x + 2, pad + width_y : pad + width_y + 1, :] = corner_high_ref[1:2]

    def neighbours(ref, at):
        return (
            along_z(ref[at, inner, :])
            + (ref[at, pad - 1 : pad + width_y - 1, :] + ref[at, pad + 1 : pad + width_y + 1, :])
            + (ref[at - 1, inner, :] + ref[at + 1, inner, :])
        )

    group = 6

    def first(i, _):
        for j in range(group):
            at = i * group + j
            near_ref[at, inner, :] = neighbours(wide_ref, at + 1)
        return 0

    total = width_x + 2
    while total % group:
        group -= 1
    lax.fori_loop(0, total // group, first, 0)
    near_ref[0, inner, :] = near_ref[0, inner, :] * inside_ref[0]
    near_ref[width_x + 1, inner, :] = near_ref[width_x + 1, inner, :] * inside_ref[1]
    near_ref[1 : width_x + 1, pad - 1, :] = inside_ref[2] * (
        along_z(ylow_ref[1])
        + along_rows(ylow_ref[1], corner_low_ref[0:1], corner_high_ref[0:1])
        + ylow_ref[0]
        + edge_low_ref[...]
    )
    near_ref[1 : width_x + 1, pad + width_y, :] = inside_ref[3] * (
        along_z(yhigh_ref[0])
        + along_rows(yhigh_ref[0], corner_low_ref[1:2], corner_high_ref[1:2])
        + yhigh_ref[1]
        + edge_high_ref[...]
    )

    def second(i, _):
        for j in range(planes):
            x = i * planes + j
            out_ref[x] = (
                (own * first_own + scale) * source_ref[x]
                + (own * spread + spread * first_own) * near_ref[x + 1, inner, :]
                + (spread * spread) * neighbours(near_ref, x + 1)
            )
        at = pl.ds(i * planes, planes)
        pltpu.make_async_copy(out_ref.at[at], out_at.at[at], sems.at[i]).start()
        return 0

    lax.fori_loop(0, width_x // planes, second, 0)

    def settle(i, _):
        at = pl.ds(i * planes, planes)
        pltpu.make_async_copy(out_ref.at[at], out_at.at[at], sems.at[i]).wait()
        return 0

    lax.fori_loop(0, width_x // planes, settle, 0)


def reply_kernel(rank_ref, owner_ref, reply_ref, out_ref):
    devices, capacity = reply_ref.shape
    count = rank_ref.shape[1]
    at_rank = (lax.broadcasted_iota(I32, (capacity, count), 0) == rank_ref[...]).astype(F32).astype(BF16)
    total = jnp.zeros((devices, count), F32)
    for piece in parts(reply_ref[...], 3):
        total = total + dot_nn(piece, at_rank)
    match = lax.broadcasted_iota(I32, (devices, count), 0) == owner_ref[...]
    out_ref[...] = jnp.sum(jnp.where(match, total, 0.0), axis=0, keepdims=True)


def shift(x, axis, up):
    count = lax.axis_size(axis)
    pairs = [(i, i + 1) if up else (i + 1, i) for i in range(count - 1)]
    return lax.ppermute(x, axis, pairs)


def body(velocity, adjoint, coupling, jac_weight, owner, local_block, offsets, margin, filtered):
    both = ("brick", "dom")
    brick_count = lax.axis_size("brick")
    dom_count = lax.axis_size("dom")
    devices = brick_count * dom_count
    count = owner.shape[0]
    width_x, width_y, depth = filtered.shape
    capacity = max(2, 2 * count // devices)
    slots = devices * capacity
    shape = jax.ShapeDtypeStruct
    vmem = pl.BlockSpec(memory_space=pltpu.VMEM)
    smem = pl.BlockSpec(memory_space=pltpu.SMEM)
    hbm = pl.BlockSpec(memory_space=pltpu.HBM)

    owner_row = owner.reshape(1, count)
    stride = capacity + -(-2 * capacity // depth)
    lanes = 128
    turned = (count // lanes, lanes, offsets.shape[0])
    outgoing, rank = pl.pallas_call(
        functools.partial(send_kernel, devices=devices, capacity=capacity),
        out_shape=(shape((devices * stride, depth), F32), shape((1, count), I32)),
        in_specs=[hbm] * 8,
        out_specs=(vmem, vmem),
        scratch_shapes=[
            pltpu.VMEM((1, count), I32),
            pltpu.VMEM((1, count), I32),
            pltpu.VMEM((1, count), F32),
            pltpu.VMEM(velocity.shape, BF16),
            pltpu.VMEM(adjoint.shape, BF16),
            pltpu.VMEM(coupling.shape, BF16),
            pltpu.VMEM(offsets.shape, I32),
            pltpu.VMEM(margin.shape, F32),
            pltpu.VMEM(turned, I32),
            pltpu.VMEM(turned, I32),
            pltpu.VMEM(turned, F32),
            pltpu.VMEM(turned, F32),
            pltpu.VMEM((count * depth // lanes, lanes), F32),
            pltpu.VMEM((2 * depth, count), BF16),
            pltpu.SemaphoreType.DMA((8,)),
        ],
        compiler_params=params(VMEM_WHOLE),
        name="send",
    )(
        owner_row,
        local_block.reshape(1, count),
        jac_weight.reshape(1, count),
        velocity,
        adjoint,
        coupling,
        offsets,
        margin,
    )
    got = lax.all_to_all(
        outgoing.reshape(devices, 1, stride * depth), both, split_axis=0, concat_axis=0, tiled=True
    ).reshape(devices * stride, depth)
    source, yfirst, ylast, density = pl.pallas_call(
        functools.partial(owner_kernel, capacity=capacity),
        out_shape=(
            shape((width_x, width_y, depth), F32),
            shape((2, width_x, depth), F32),
            shape((2, width_x, depth), F32),
            shape((devices, 1, capacity), F32),
        ),
        scratch_shapes=[
            pltpu.VMEM((devices, depth), F32),
            pltpu.VMEM((devices, depth), I32),
            pltpu.VMEM((slots, depth), F32),
            pltpu.VMEM((slots, 2 * depth), BF16),
            pltpu.VMEM((width_y, slots), BF16),
            pltpu.SMEM((devices, depth), I32),
            pltpu.SemaphoreType.DMA,
        ],
        compiler_params=params(),
        name="owners",
    )(got, filtered.reshape(width_x * width_y, depth))

    reply = lax.all_to_all(
        density, both, split_axis=0, concat_axis=0, tiled=True
    )
    element_density = pl.pallas_call(
        reply_kernel,
        out_shape=shape((1, count), F32),
        compiler_params=params(),
        name="reply",
    )(rank, owner_row, reply.reshape(devices, capacity))

    ylow = shift(ylast, "dom", True)
    yhigh = shift(yfirst, "dom", False)
    top = jnp.concatenate(
        [source[width_x - 2], source[width_x - 1], ylow[1, width_x - 1 :], yhigh[0, width_x - 1 :], jnp.zeros((6, depth), F32)]
    )
    bottom = jnp.concatenate(
        [source[0], source[1], ylow[1, :1], yhigh[0, :1], jnp.zeros((6, depth), F32)]
    )
    from_low = shift(top, "brick", True)
    from_high = shift(bottom, "brick", False)
    brick, dom = lax.axis_index("brick"), lax.axis_index("dom")
    inside = jnp.stack([brick > 0, brick < brick_count - 1, dom > 0, dom < dom_count - 1]).astype(F32)
    result = pl.pallas_call(
        sweep_kernel,
        out_shape=shape((width_x, width_y, depth), F32),
        in_specs=[smem] + [vmem] * 9,
        out_specs=hbm,
        scratch_shapes=[
            pltpu.VMEM((width_x + 4, width_y + 16, depth), F32),
            pltpu.VMEM((width_x + 2, width_y + 16, depth), F32),
            pltpu.VMEM((width_x, width_y, depth), F32),
            pltpu.SemaphoreType.DMA((width_x // 8,)),
        ],
        compiler_params=params(),
        name="sweep",
    )(
        inside,
        source,
        from_low[: 2 * width_y].reshape(2, width_y, depth),
        from_high[: 2 * width_y].reshape(2, width_y, depth),
        ylow,
        yhigh,
        yfirst[0],
        ylast[1],
        from_low[2 * width_y : 2 * width_y + 8],
        from_high[2 * width_y : 2 * width_y + 8],
    )
    return (result, element_density.reshape(count))


def solution(mesh):
    return jax.shard_map(
        body,
        mesh=mesh,
        in_specs=(
            P(None, None, ("brick", "dom")),
            P(None, None, ("brick", "dom")),
            P(),
            P(("brick", "dom")),
            P(("brick", "dom"), None),
            P(("brick", "dom")),
            P(None, ("brick", "dom")),
            P(None, ("brick", "dom")),
            P("brick", "dom", None),
        ),
        out_specs=(P("brick", "dom", None), P(("brick", "dom"))),
        check_vma=False,
    )
```

time: 102 us -> 81.9 us (0.80)
  the two profiles are of different devices: /device:TPU:0 before, /device:TPU:5 now
where the time goes in v2:
time: 81.9 us; the launch traced here: 81.5 us
  waiting for transfers between devices  33.3 us (41%)
  Pallas kernels  23.7 us (29%)
  starting transfers between devices  21.9 us (27%)
  local copies, waits for them, and re-layouts  1.7 us (2%)
    all_to_all x1, waiting for transfers between devices, body(): lax.all_to_all(outgoing.reshape(devices, 1, stride * depth), both, split_...  26.7 us
    ppermute x4, starting transfers between devices, shift(): return lax.ppermute(x, axis, pairs)  12 us
    pallas_call x1, Pallas kernels, body(): pl.pallas_call(functools.partial(owner_kernel, capacity=capacity), out_sh...  9.35 us
    pallas_call x1, Pallas kernels, body(): pl.pallas_call(functools.partial(send_kernel, devices=devices, capacity=c...  8.34 us
    ppermute x4, waiting for transfers between devices, shift(): return lax.ppermute(x, axis, pairs)  6.55 us
    all_to_all x1, starting transfers between devices, body(): lax.all_to_all(outgoing.reshape(devices, 1, stride * depth), both, split_...  6.42 us
    pallas_call x1, Pallas kernels, body(): pl.pallas_call(sweep_kernel, out_shape=shape((width_x, width_y, depth), F...  5.23 us
    all_to_all x1, starting transfers between devices, body(): lax.all_to_all(density, both, split_axis=0, concat_axis=0, tiled=True)  3.53 us
  transfers between devices with their start and end apart: 6, of which 3 were waited for; matrix products, arithmetic and copies ran while one was open for 0% of the time, Pallas kernels for 1%

profile of v2, /device:TPU:5, one launch (start us, length us, event | category | flops | bytes accessed | tf_op | source)
XLA Modules:
  0.0 81.5 jit_solution(5792382759451885648)
XLA Ops:
  0.6 8.3 %send.1 = (f32[2080,128]{1,0:T(8,128)}, s32[1,1024]{1,0:T(1,128)}) custom-call(s32[1,1024]{1,0:T(1,128)} %bitcast.39, s32[1,1024]{1,0:T(1,128)} %bitcast.42, f32[1,1024]{1,0:T(1,128)} %bitcast.43, bf16[3,27,1024]{2,1,0:T(8,128)(2,1)} %vel_at.1, bf16[3,27,1024]{2,1,0:T(8,128)(2,1)} %adj_at.1, bf16[27,27]{1,0:T(8,128)(2,1)} %coup_at.1, s32[128,1024]{1,0:T(8,128)} %off_at.1, ...), custom_call_target="tpu_custom_call" | custom-call | tf_op jit(solution)/shard_map/send/pallas_call | solution.py:388
  9.0 6.4 %all-to-all-start = ((f32[32,1,8320]{2,1,0:T(1,128)}), f32[32,1,8320]{2,1,0:T(1,128)S(1)}, u32[]{:S(2)}, u32[]{:S(2)}) async-start(f32[32,1,8320]{2,1,0:T(1,128)} %bitcast.41), calls=%async_computation | async-start | bytes 2129920 | tf_op jit(solution)/shard_map/all_to_all | solution.py:422
  15.4 0.0 copy-start.1
  15.4 0.0 copy-start.2
  15.4 0.1 add_convert_fusion.inside_ref
  15.5 26.7 %all-to-all-done = f32[32,1,8320]{2,1,0:T(1,128)S(1)} async-done(((f32[32,1,8320]{2,1,0:T(1,128)}), f32[32,1,8320]{2,1,0:T(1,128)S(1)}, u32[]{:S(2)}, u32[]{:S(2)}) %all-to-all-start) | async-done | bytes 1064992 | tf_op jit(solution)/shard_map/all_to_all | solution.py:422
  42.3 0.0 copy-start
  42.3 1.6 %copy-done = f32[64,64,128]{2,1,0:T(8,128)S(1)} copy-done((f32[64,64,128]{2,1,0:T(8,128)S(1)}, f32[64,64,128]{2,1,0:T(8,128)}, u32[]{:S(2)}) %copy-start) | copy-done | bytes 2097176
  43.9 9.3 %owners.1 = (f32[64,64,128]{2,1,0:T(8,128)S(1)}, f32[2,64,128]{2,1,0:T(8,128)S(1)}, f32[2,64,128]{2,1,0:T(8,128)S(1)}, f32[32,1,64]{2,1,0:T(1,128)}) custom-call(f32[2080,128]{1,0:T(8,128)S(1)} %bitcast.34, f32[4096,128]{1,0:T(8,128)S(1)} %bitcast.35), custom_call_target="tpu_custom_call" | custom-call | tf_op jit(solution)/shard_map/owners/pallas_call | solution.py:425
  53.2 3.5 %all-to-all-start.1 = ((f32[32,1,64]{2,1,0:T(1,128)}), f32[32,1,64]{2,1,0:T(1,128)S(1)}, u32[]{:S(2)}, u32[]{:S(2)}) async-start(f32[32,1,64]{2,1,0:T(1,128)} %get-tuple-element.13), calls=%async_computation.1 | async-start | bytes 32768 | tf_op jit(solution)/shard_map/all_to_all | solution.py:446
  56.8 3.1 %collective-permute-start = (f32[2,64,128]{2,1,0:T(8,128)S(1)}, f32[2,64,128]{2,1,0:T(8,128)S(1)}, u32[]{:S(2)}, u32[]{:S(2)}) collective-permute-start(f32[2,64,128]{2,1,0:T(8,128)S(1)} %get-tuple-element.10), channel_id=1, source_target_pairs={{0,1},{1,2},{2,3},{3,4},{4,5},{5,6},{6,7},{8,9},{9,10},{10,11},{11... | collective-permute-start | bytes 196616 | tf_op jit(solution)/shard_map/ppermute | solution.py:367
  59.9 2.2 %collective-permute-start.1 = (f32[2,64,128]{2,1,0:T(8,128)S(1)}, f32[2,64,128]{2,1,0:T(8,128)S(1)}, u32[]{:S(2)}, u32[]{:S(2)}) collective-permute-start(f32[2,64,128]{2,1,0:T(8,128)S(1)} %get-tuple-element.11), channel_id=1, source_target_pairs={{1,0},{2,1},{3,2},{4,3},{5,4},{6,5},{7,6},{9,8},{10,9},{11,10},{12... | collective-permute-start | bytes 196616 | tf_op jit(solution)/shard_map/ppermute | solution.py:367
  62.1 0.0 collective-permute-done.ylow_ref
  62.1 3.7 %collective-permute-done.1.yhigh_ref = f32[2,64,128]{2,1,0:T(8,128)S(1)} collective-permute-done((f32[2,64,128]{2,1,0:T(8,128)S(1)}, f32[2,64,128]{2,1,0:T(8,128)S(1)}, u32[]{:S(2)}, u32[]{:S(2)}) %collective-permute-start.1) | collective-permute-done | bytes 65568 | tf_op jit(solution)/shard_map/ppermute | solution.py:367
  65.8 4.8 %collective-permute-start.2 = (f32[136,128]{1,0:T(8,128)S(1)}, f32[136,128]{1,0:T(8,128)S(1)}, u32[]{:S(2)}, u32[]{:S(2)}) collective-permute-start(f32[136,128]{1,0:T(8,128)S(1)} %concatenate.6), channel_id=1, source_target_pairs={{0,8},{8,16},{16,24},{1,9},{9,17},{17,25},{2,10},{10,18},{18,26},{... | collective-permute-start | bytes 208904 | tf_op jit(solution)/shard_map/ppermute | solution.py:367
  70.6 1.9 %collective-permute-start.3 = (f32[136,128]{1,0:T(8,128)S(1)}, f32[136,128]{1,0:T(8,128)S(1)}, u32[]{:S(2)}, u32[]{:S(2)}) collective-permute-start(f32[136,128]{1,0:T(8,128)S(1)} %concatenate.7), channel_id=1, source_target_pairs={{8,0},{16,8},{24,16},{9,1},{17,9},{25,17},{10,2},{18,10},{26,18},{... | collective-permute-start | bytes 208904 | tf_op jit(solution)/shard_map/ppermute | solution.py:367
  72.6 0.0 all-to-all-done.1
  72.6 0.0 copy-done.1
  72.6 0.0 copy-done.2
  72.6 0.8 reply.1
  73.4 0.0 collective-permute-done.2
  73.4 2.8 %collective-permute-done.3 = f32[136,128]{1,0:T(8,128)S(1)} collective-permute-done((f32[136,128]{1,0:T(8,128)S(1)}, f32[136,128]{1,0:T(8,128)S(1)}, u32[]{:S(2)}, u32[]{:S(2)}) %collective-permute-start.3) | collective-permute-done | bytes 69664 | tf_op jit(solution)/shard_map/ppermute | solution.py:367
  76.3 5.2 %sweep.1 = f32[64,64,128]{2,1,0:T(8,128)} custom-call(f32[4]{0:T(128)S(1)} %add_convert_fusion.inside_ref, f32[64,64,128]{2,1,0:T(8,128)S(1)} %get-tuple-element.9.source_ref, f32[2,64,128]{2,1,0:T(8,128)S(1)} %bitcast.36, f32[2,64,128]{2,1,0:T(8,128)S(1)} %bitcast.37, f32[2,64,128]{2,1,0:T(8,128)S(1)} %collective-permute-done.ylow_ref, ...), custom_call_target="tpu_custom_call" | custom-call | tf_op jit(solution)/shard_map/sweep/pallas_call | solution.py:468
  (11 shorter events, 0.1 us)
Async XLA Ops:
  9.0 33.3 %all-to-all-start = ((f32[32,1,8320]{2,1,0:T(1,128)}), f32[32,1,8320]{2,1,0:T(1,128)S(1)}, u32[]{:S(2)}, u32[]{:S(2)}) async-start(f32[32,1,8320]{2,1,0:T(1,128)} %bitcast.41), calls=%async_computation | async-start | bytes 2129920 | tf_op jit(solution)/shard_map/all_to_all | solution.py:422
  15.4 57.2 %copy-start.1 = (s32[1024,1]{0,1:T(1,128)S(1)}, s32[1024,1]{0,1:T(1,128)}, u32[]{:S(2)}) copy-start(s32[1024,1]{0,1:T(1,128)} %param.13) | copy-start | bytes 12292
  15.4 57.2 %copy-start.2 = (s32[1,1024]{1,0:T(1,128)S(1)}, s32[1,1024]{1,0:T(1,128)}, u32[]{:S(2)}) copy-start(s32[1,1024]{1,0:T(1,128)} %get-tuple-element.12.rank_ref) | copy-start | bytes 12292
  42.3 1.6 %copy-start = (f32[64,64,128]{2,1,0:T(8,128)S(1)}, f32[64,64,128]{2,1,0:T(8,128)}, u32[]{:S(2)}) copy-start(f32[64,64,128]{2,1,0:T(8,128)} %param.17) | copy-start | bytes 6291460
  53.2 19.4 %all-to-all-start.1 = ((f32[32,1,64]{2,1,0:T(1,128)}), f32[32,1,64]{2,1,0:T(1,128)S(1)}, u32[]{:S(2)}, u32[]{:S(2)}) async-start(f32[32,1,64]{2,1,0:T(1,128)} %get-tuple-element.13), calls=%async_computation.1 | async-start | bytes 32768 | tf_op jit(solution)/shard_map/all_to_all | solution.py:446
  56.8 5.3 %collective-permute-start = (f32[2,64,128]{2,1,0:T(8,128)S(1)}, f32[2,64,128]{2,1,0:T(8,128)S(1)}, u32[]{:S(2)}, u32[]{:S(2)}) collective-permute-start(f32[2,64,128]{2,1,0:T(8,128)S(1)} %get-tuple-element.10), channel_id=1, source_target_pairs={{0,1},{1,2},{2,3},{3,4},{4,5},{5,6},{6,7},{8,9},{9,10},{10,11},{11... | collective-permute-start | bytes 196616 | tf_op jit(solution)/shard_map/ppermute | solution.py:367
  59.9 5.9 %collective-permute-start.1 = (f32[2,64,128]{2,1,0:T(8,128)S(1)}, f32[2,64,128]{2,1,0:T(8,128)S(1)}, u32[]{:S(2)}, u32[]{:S(2)}) collective-permute-start(f32[2,64,128]{2,1,0:T(8,128)S(1)} %get-tuple-element.11), channel_id=1, source_target_pairs={{1,0},{2,1},{3,2},{4,3},{5,4},{6,5},{7,6},{9,8},{10,9},{11,10},{12... | collective-permute-start | bytes 196616 | tf_op jit(solution)/shard_map/ppermute | solution.py:367
  65.8 7.6 %collective-permute-start.2 = (f32[136,128]{1,0:T(8,128)S(1)}, f32[136,128]{1,0:T(8,128)S(1)}, u32[]{:S(2)}, u32[]{:S(2)}) collective-permute-start(f32[136,128]{1,0:T(8,128)S(1)} %concatenate.6), channel_id=1, source_target_pairs={{0,8},{8,16},{16,24},{1,9},{9,17},{17,25},{2,10},{10,18},{18,26},{... | collective-permute-start | bytes 208904 | tf_op jit(solution)/shard_map/ppermute | solution.py:367
  70.6 5.6 %collective-permute-start.3 = (f32[136,128]{1,0:T(8,128)S(1)}, f32[136,128]{1,0:T(8,128)S(1)}, u32[]{:S(2)}, u32[]{:S(2)}) collective-permute-start(f32[136,128]{1,0:T(8,128)S(1)} %concatenate.7), channel_id=1, source_target_pairs={{8,0},{16,8},{24,16},{9,1},{17,9},{25,17},{10,2},{18,10},{26,18},{... | collective-permute-start | bytes 208904 | tf_op jit(solution)/shard_map/ppermute | solution.py:367

commit v3 on v2

--- a/solution.py
+++ b/solution.py
@@ -52,10 +52,10 @@
     return copies
 
 
-def send_kernel(owner_at, block_at, jac_at, vel_at, adj_at, coup_at, off_at, mar_at, out_ref, rank_ref, owner_ref, block_ref, jac_ref, vel_ref, adj_ref, coup_ref, off_ref, mar_ref, high_ref, low_ref, first_ref, second_ref, hist_ref, map_ref, sems, *, devices, capacity):
+def send_kernel(owner_at, block_at, jac_at, vel_at, adj_at, coup_at, off_at, mar_at, out_at, rank_ref, owner_ref, block_ref, jac_ref, vel_ref, adj_ref, coup_ref, off_ref, mar_ref, high_ref, low_ref, first_ref, second_ref, hist_ref, map_ref, out_ref, sems, *, devices, capacity):
     copies = fetch(
-        [off_at, mar_at, owner_at, block_at, jac_at, vel_at, adj_at, coup_at],
-        [off_ref, mar_ref, owner_ref, block_ref, jac_ref, vel_ref, adj_ref, coup_ref],
+        [owner_at, block_at, jac_at, vel_at, adj_at, coup_at, off_at, mar_at],
+        [owner_ref, block_ref, jac_ref, vel_ref, adj_ref, coup_ref, off_ref, mar_ref],
         sems,
     )
     slots, depth = out_ref.shape
@@ -67,7 +67,7 @@
     before = lax.broadcasted_iota(I32, (group, 2 * group), 0)
     after = lax.broadcasted_iota(I32, (group, 2 * group), 1)
     sums = ((before < after) | (after >= group)).astype(F32).astype(BF16)
-    for copy in copies[2:]:
+    for copy in copies[:6]:
         copy.wait()
     owner = owner_ref[...]
     carry = jnp.zeros((devices, group), F32)
@@ -105,7 +105,7 @@
     sets = count // group
     lows = group // sets
     highs = depth // lows
-    for copy in copies[:2]:
+    for copy in copies[6:]:
         copy.wait()
     for b in range(sets):
         off = off_ref[:, b * group : (b + 1) * group].T
@@ -157,14 +157,23 @@
 
     place = owner * stride + rank
     tile = slots // 4
+    stores = []
     for at in range(0, slots, tile):
         row_of = lax.broadcasted_iota(I32, (tile, count), 0) + at
         here = (row_of == place).astype(F32).astype(BF16)
         moved = dot_nt(here, map_ref[...])
         out_ref[at : at + tile, :] = moved[:, :depth] + moved[:, depth:]
-    for d in range(devices):
-        row = d * stride + capacity
-        out_ref[row : row + 1, :] = meta[d : d + 1, :]
+        for d in range(devices):
+            row = d * stride + capacity
+            if at <= row < at + tile:
+                out_ref[row : row + 1, :] = meta[d : d + 1, :]
+        store = pltpu.make_async_copy(
+            out_ref.at[pl.ds(at, tile)], out_at.at[pl.ds(at, tile)], sems.at[at // tile]
+        )
+        store.start()
+        stores.append(store)
+    for store in stores:
+        store.wait()
 
 
 def constants():
@@ -172,12 +181,17 @@
     return base, base + jnp.tanh(jnp.full((1, 1), sharpness * (1.0 - threshold), F32))
 
 
-def owner_kernel(got_ref, field_ref, source_ref, ylow_ref, yhigh_ref, dens_ref, meta_ref, block_ref, found_ref, val_ref, y_ref, number_ref, sem, *, capacity):
+def slope_of(field, inverse):
+    tangent = jnp.tanh(sharpness * (field - threshold))
+    return sharpness * inverse * (1.0 - tangent * tangent)
+
+
+def owner_kernel(odd_ref, got_ref, field_ref, val_at, y_ref, x_ref, yeven_ref, yodd_ref, dens_ref, val_ref, meta_ref, block_ref, found_ref, number_ref, sems, *, capacity, width_y):
     devices = dens_ref.shape[0]
     stride = got_ref.shape[0] // devices
     depth = got_ref.shape[1]
     rows = devices * capacity
-    width_x, width_y, _ = source_ref.shape
+    width_x = field_ref.shape[0] // width_y
     group = 128
 
     for d in range(devices):
@@ -185,7 +199,7 @@
         meta_ref[d : d + 1, :] = got_ref[row : row + 1, :]
     meta = meta_ref[...]
     block_ref[...] = meta.astype(I32)
-    copy = pltpu.make_async_copy(block_ref, number_ref, sem)
+    copy = pltpu.make_async_copy(block_ref, number_ref, sems.at[0])
     copy.start()
     prods = meta.T
     joined = group // capacity
@@ -198,7 +212,10 @@
     y_of = lax.broadcasted_iota(I32, (width_y, group), 0)
     for k, part in enumerate(index):
         y_ref[:, k * group : (k + 1) * group] = (y_of == part % width_y).astype(F32).astype(BF16)
-    x_row = jnp.concatenate(index, axis=1) // width_y
+    joint = jnp.concatenate(index, axis=1)
+    x_row = joint // width_y
+    y_row = joint % width_y
+    x_ref[...] = x_row
     copy.wait()
 
     def look(d, _):
@@ -229,27 +246,25 @@
         val_ref[at, :depth] = high
         val_ref[at, depth:] = low
 
-    planes = 16
-    tile = planes * width_y
-
-    def step(i, _):
-        here = []
-        for j in range(planes):
-            at_x = (x_row == i * planes + j).astype(F32)
-            here.append(y_ref[...] * jnp.broadcast_to(at_x, (width_y, rows)).astype(BF16))
-        summed = dot_nn(jnp.concatenate(here, axis=0), val_ref[...])
-        at = pl.ds(pl.multiple_of(i * tile, tile), tile)
-        tangent = jnp.tanh(sharpness * (field_ref[at, :] - threshold))
-        slope = sharpness * inverse * (1.0 - tangent * tangent)
-        source = (summed[:, :depth] + summed[:, depth:]) * slope
-        source_ref[pl.ds(i * planes, planes), :, :] = source.reshape(planes, width_y, depth)
-        return 0
-
-    lax.fori_loop(0, width_x // planes, step, 0)
-    ylow_ref[0] = source_ref[:, 0, :]
-    ylow_ref[1] = source_ref[:, 1, :]
-    yhigh_ref[0] = source_ref[:, width_y - 2, :]
-    yhigh_ref[1] = source_ref[:, width_y - 1, :]
+    store = pltpu.make_async_copy(val_ref, val_at, sems.at[1])
+    store.start()
+
+    x_hot = (lax.broadcasted_iota(I32, (width_x, rows), 0) == x_row).astype(F32).astype(BF16)
+    ys = (0, 1, width_y - 2, width_y - 1)
+    here = [
+        x_hot * jnp.broadcast_to((y_row == y).astype(F32), (width_x, rows)).astype(BF16) for y in ys
+    ]
+    summed = dot_nn(jnp.concatenate(here, axis=0), val_ref[...])
+    summed = summed[:, :depth] + summed[:, depth:]
+    faces = []
+    for i, y in enumerate(ys):
+        field = field_ref[pl.ds(y, width_x, stride=width_y), :]
+        faces.append(summed[i * width_x : (i + 1) * width_x] * slope_of(field, inverse))
+    odd = odd_ref[1] == 1
+    for i in range(2):
+        yeven_ref[i] = jnp.where(odd, faces[i], faces[2 + i])
+        yodd_ref[i] = jnp.where(odd, faces[2 + i], faces[i])
+    store.wait()
 
 
 def along_z(x):
@@ -260,7 +275,7 @@
     return up + down
 
 
-def along_rows(x, low, high):
+def along_rows(x, low=0.0, high=0.0):
     row = lax.broadcasted_iota(I32, x.shape, 0)
     count = x.shape[0]
     up = jnp.where(row == 0, jnp.broadcast_to(low, x.shape), pltpu.roll(x, 1, 0))
@@ -268,86 +283,170 @@
     return up + down
 
 
-def sweep_kernel(inside_ref, source_ref, xlow_ref, xhigh_ref, ylow_ref, yhigh_ref, edge_low_ref, edge_high_ref, corner_low_ref, corner_high_ref, out_at, wide_ref, near_ref, out_ref, sems):
-    width_x, width_y, depth = source_ref.shape
-    pad = 8
-    inner = slice(pad, pad + width_y)
+def weights_of():
     center = 1.0 + 6.0 * radius_sq
     spread = relax * radius_sq / center
     scale = relax / center
     own = 1.0 - relax
-    first_own = own + scale
+    return own * (own + scale) + scale, own * spread + spread * (own + scale), spread * spread
+
+
+PAD = 8
+
+
+def neighbours(ref, at, inner):
+    before, after = inner.start, inner.stop
+    return (
+        along_z(ref[at, inner, :])
+        + (ref[at, before - 1 : after - 1, :] + ref[at, before + 1 : after + 1, :])
+        + (ref[at - 1, inner, :] + ref[at + 1, inner, :])
+    )
+
+
+def step_planes(width_x):
     planes = 8
-
-    def widen(i, _):
+    while width_x % planes:
+        planes //= 2
+    return planes
+
+
+def scatter_kernel(inside_ref, val_at, y_ref, x_ref, field_at, out_at, face_ref, xs_ref, ys_ref, val_ref, field_ref, wide_ref, near_ref, out_ref, sems):
+    loads = fetch([val_at, field_at], [val_ref, field_ref], sems)
+    rows = val_ref.shape[0]
+    width_x, width_y = ys_ref.shape[0], xs_ref.shape[1]
+    depth = out_ref.shape[2]
+    inner = slice(PAD, PAD + width_y)
+    _, ceiling = constants()
+    inverse = 1.0 / ceiling
+    once, near, far = weights_of()
+    planes = step_planes(width_x)
+    tile = planes * width_y
+    steps = width_x // planes
+    lead = 2 * planes + 3
+    for ref in (wide_ref, near_ref):
+        edges = (*range(lead), lead + width_x)
+        for x in edges:
+            ref[x] = jnp.zeros(ref.shape[1:], F32)
+        ref[lead : lead + width_x, 0:PAD, :] = jnp.zeros((width_x, PAD, depth), F32)
+        ref[lead : lead + width_x, PAD + width_y :, :] = jnp.zeros((width_x, PAD, depth), F32)
+    def sums(x):
+        near_ref[x, inner, :] = neighbours(wide_ref, x, inner)
+
+    def sweeps(x):
+        out_ref[x] = (
+            once * wide_ref[x, inner, :]
+            + near * near_ref[x, inner, :]
+            + far * neighbours(near_ref, x, inner)
+        )
+
+    def store(i):
         at = i * planes
-        wide_ref[pl.ds(at + 2, planes), inner, :] = source_ref[pl.ds(at, planes)]
+        return pltpu.make_async_copy(
+            out_ref.at[pl.ds(lead + at, planes)], out_at.at[pl.ds(at, planes)], sems.at[i]
+        )
+
+    def gather(i):
+        at = i * planes
+        here = []
+        for j in range(planes):
+            at_x = (x_ref[...] == at + j).astype(F32)
+            here.append(y_ref[...] * jnp.broadcast_to(at_x, (width_y, rows)).astype(BF16))
+        summed = dot_nn(jnp.concatenate(here, axis=0), val_ref[...])
+        return summed[:, :depth] + summed[:, depth:]
+
+    def spread(i, summed):
+        field = field_ref[pl.ds(pl.multiple_of(i * tile, tile), tile), :]
+        source = summed * slope_of(field, inverse)
+        wide_ref[pl.ds(lead + i * planes, planes), inner, :] = source.reshape(planes, width_y, depth)
+
+    def step(i, _):
+        at = i * planes
+        for j in range(planes):
+            sweeps(lead + at - 2 * planes - 2 + j)
+        for j in range(planes):
+            sums(lead + at - planes - 1 + j)
+        near_ref[lead - 1, inner, :] = jnp.zeros((width_y, depth), F32)
+        spread(i, gather(i))
+
+        def done():
+            store(i - 3).start()
+
+        pl.when(i >= 3)(done)
         return 0
 
-    lax.fori_loop(0, width_x // planes, widen, 0)
-    wide_ref[0:2, inner, :] = xlow_ref[...]
-    wide_ref[width_x + 2 : width_x + 4, inner, :] = xhigh_ref[...]
-    wide_ref[2 : width_x + 2, pad - 1, :] = ylow_ref[1]
-    wide_ref[2 : width_x + 2, pad + width_y, :] = yhigh_ref[0]
-    wide_ref[1, pad - 1 : pad, :] = corner_low_ref[0:1]
-    wide_ref[1, pad + width_y : pad + width_y + 1, :] = corner_low_ref[1:2]
-    wide_ref[width_x + 2, pad - 1 : pad, :] = corner_high_ref[0:1]
-    wide_ref[width_x + 2, pad + width_y : pad + width_y + 1, :] = corner_high_ref[1:2]
-
-    def neighbours(ref, at):
-        return (
-            along_z(ref[at, inner, :])
-            + (ref[at, pad - 1 : pad + width_y - 1, :] + ref[at, pad + 1 : pad + width_y + 1, :])
-            + (ref[at - 1, inner, :] + ref[at + 1, inner, :])
-        )
-
-    group = 6
-
-    def first(i, _):
-        for j in range(group):
-            at = i * group + j
-            near_ref[at, inner, :] = neighbours(wide_ref, at + 1)
-        return 0
-
-    total = width_x + 2
-    while total % group:
-        group -= 1
-    lax.fori_loop(0, total // group, first, 0)
-    near_ref[0, inner, :] = near_ref[0, inner, :] * inside_ref[0]
-    near_ref[width_x + 1, inner, :] = near_ref[width_x + 1, inner, :] * inside_ref[1]
-    near_ref[1 : width_x + 1, pad - 1, :] = inside_ref[2] * (
-        along_z(ylow_ref[1])
-        + along_rows(ylow_ref[1], corner_low_ref[0:1], corner_high_ref[0:1])
-        + ylow_ref[0]
-        + edge_low_ref[...]
-    )
-    near_ref[1 : width_x + 1, pad + width_y, :] = inside_ref[3] * (
-        along_z(yhigh_ref[0])
-        + along_rows(yhigh_ref[0], corner_low_ref[1:2], corner_high_ref[1:2])
-        + yhigh_ref[1]
-        + edge_high_ref[...]
-    )
-
-    def second(i, _):
-        for j in range(planes):
-            x = i * planes + j
-            out_ref[x] = (
-                (own * first_own + scale) * source_ref[x]
-                + (own * spread + spread * first_own) * near_ref[x + 1, inner, :]
-                + (spread * spread) * neighbours(near_ref, x + 1)
-            )
-        at = pl.ds(i * planes, planes)
-        pltpu.make_async_copy(out_ref.at[at], out_at.at[at], sems.at[i]).start()
-        return 0
-
-    lax.fori_loop(0, width_x // planes, second, 0)
-
-    def settle(i, _):
-        at = pl.ds(i * planes, planes)
-        pltpu.make_async_copy(out_ref.at[at], out_at.at[at], sems.at[i]).wait()
-        return 0
-
-    lax.fori_loop(0, width_x // planes, settle, 0)
+    loads[0].wait()
+    summed = gather(0)
+    loads[1].wait()
+    spread(0, summed)
+    lax.fori_loop(1, steps, step, 0)
+    for x in range((steps - 1) * planes - 1, width_x):
+        sums(lead + x)
+    for x in range((steps - 2) * planes - 2, width_x):
+        sweeps(lead + x)
+    for i in range(max(0, steps - 3), steps):
+        store(i).start()
+    for k, x in enumerate((0, 1, width_x - 2, width_x - 1)):
+        face_ref[k] = wide_ref[lead + x, inner, :]
+        xs_ref[k] = out_ref[lead + x]
+    xs_ref[0] = xs_ref[0] + (far * inside_ref[0]) * face_ref[0]
+    xs_ref[3] = xs_ref[3] + (far * inside_ref[1]) * face_ref[3]
+    block = slice(lead, lead + width_x)
+    ys_ref[:, 0:PAD, :] = out_ref[block, 0:PAD, :]
+    ys_ref[:, PAD : 2 * PAD, :] = out_ref[block, width_y - PAD :, :]
+    for y, at, side in ((0, 0, 2), (width_y - 1, 2 * PAD - 1, 3)):
+        add = (far * inside_ref[side]) * wide_ref[block, PAD + y, :]
+        ys_ref[:, at, :] = ys_ref[:, at, :] + add
+        for k, x in enumerate((0, 1, width_x - 2, width_x - 1)):
+            row = slice(y, y + 1)
+            xs_ref[k, row, :] = xs_ref[k, row, :] + add[x : x + 1]
+    for i in range(steps):
+        store(i).wait()
+
+
+def border_kernel(inside_ref, odd_ref, partial_at, xs_ref, ys_ref, xeven_ref, xodd_ref, yeven_ref, yodd_ref, out_at, xwork_ref, ywork_ref, sems):
+    width_x, _, depth = ys_ref.shape
+    width_y = xs_ref.shape[1]
+    _, near, far = weights_of()
+
+    def pick(odd, even, other):
+        return jnp.where(odd, even, other), jnp.where(odd, other, even)
+
+    xodd, yodd = odd_ref[0] == 1, odd_ref[1] == 1
+    xlow, xhigh = pick(xodd, xeven_ref[...], xodd_ref[...])
+    ylow, yhigh = pick(yodd, yeven_ref[...], yodd_ref[...])
+    low_corners = xlow[2 * width_y : 2 * width_y + 2]
+    high_corners = xhigh[2 * width_y : 2 * width_y + 2]
+
+    def layer(halo, beyond, inside, low, high):
+        ring = inside * (along_z(halo) + along_rows(halo, low, high) + beyond)
+        return near * halo + far * (along_z(halo) + along_rows(halo) + ring), far * halo
+
+    def two(layers, width):
+        return layers[:width], layers[width : 2 * width]
+
+    beyond, halo = two(xlow, width_y)
+    xlow = layer(halo, beyond, inside_ref[0], low_corners[0:1], low_corners[1:2])
+    halo, beyond = two(xhigh, width_y)
+    xhigh = layer(halo, beyond, inside_ref[1], high_corners[0:1], high_corners[1:2])
+    ylow = layer(ylow[1], ylow[0], inside_ref[2], low_corners[0:1], high_corners[0:1])
+    yhigh = layer(yhigh[0], yhigh[1], inside_ref[3], low_corners[1:2], high_corners[1:2])
+    ywork_ref[...] = ys_ref[...]
+    for y, add in ((0, ylow[0]), (1, ylow[1]), (2 * PAD - 2, yhigh[1]), (2 * PAD - 1, yhigh[0])):
+        ywork_ref[:, y, :] = ywork_ref[:, y, :] + add
+    for k, (x, add) in enumerate(((0, xlow[0]), (1, xlow[1]), (width_x - 2, xhigh[1]), (width_x - 1, xhigh[0]))):
+        xwork_ref[k] = xs_ref[k] + add
+        for y, more in ((0, ylow[0]), (1, ylow[1]), (width_y - 2, yhigh[1]), (width_y - 1, yhigh[0])):
+            row = slice(y, y + 1)
+            xwork_ref[k, row, :] = xwork_ref[k, row, :] + more[x : x + 1]
+    middle = pl.ds(2, width_x - 4)
+    stores = [
+        (xwork_ref.at[pl.ds(0, 2)], out_at.at[pl.ds(0, 2)]),
+        (xwork_ref.at[pl.ds(2, 2)], out_at.at[pl.ds(width_x - 2, 2)]),
+        (ywork_ref.at[middle, pl.ds(0, PAD)], out_at.at[middle, pl.ds(0, PAD)]),
+        (ywork_ref.at[middle, pl.ds(PAD, PAD)], out_at.at[middle, pl.ds(width_y - PAD, PAD)]),
+    ]
+    for store in fetch([a for a, _ in stores], [b for _, b in stores], sems):
+        store.wait()
 
 
 def reply_kernel(rank_ref, owner_ref, reply_ref, out_ref):
@@ -361,10 +460,10 @@
     out_ref[...] = jnp.sum(jnp.where(match, total, 0.0), axis=0, keepdims=True)
 
 
-def shift(x, axis, up):
+def swap(x, axis, odd):
     count = lax.axis_size(axis)
-    pairs = [(i, i + 1) if up else (i + 1, i) for i in range(count - 1)]
-    return lax.ppermute(x, axis, pairs)
+    pairs = [(i, i + 1) for i in range(odd, count - 1, 2)]
+    return lax.ppermute(x, axis, pairs + [(j, i) for i, j in pairs])
 
 
 def body(velocity, adjoint, coupling, jac_weight, owner, local_block, offsets, margin, filtered):
@@ -381,6 +480,9 @@
     smem = pl.BlockSpec(memory_space=pltpu.SMEM)
     hbm = pl.BlockSpec(memory_space=pltpu.HBM)
 
+    brick, dom = lax.axis_index("brick"), lax.axis_index("dom")
+    inside = jnp.stack([brick > 0, brick < brick_count - 1, dom > 0, dom < dom_count - 1]).astype(F32)
+    odd = jnp.stack([brick % 2, dom % 2]).astype(I32)
     owner_row = owner.reshape(1, count)
     stride = capacity + -(-2 * capacity // depth)
     lanes = 128
@@ -389,7 +491,7 @@
         functools.partial(send_kernel, devices=devices, capacity=capacity),
         out_shape=(shape((devices * stride, depth), F32), shape((1, count), I32)),
         in_specs=[hbm] * 8,
-        out_specs=(vmem, vmem),
+        out_specs=(hbm, vmem),
         scratch_shapes=[
             pltpu.VMEM((1, count), I32),
             pltpu.VMEM((1, count), I32),
@@ -405,6 +507,7 @@
             pltpu.VMEM(turned, F32),
             pltpu.VMEM((count * depth // lanes, lanes), F32),
             pltpu.VMEM((2 * depth, count), BF16),
+            pltpu.VMEM((devices * stride, depth), F32),
             pltpu.SemaphoreType.DMA((8,)),
         ],
         compiler_params=params(VMEM_WHOLE),
@@ -422,30 +525,76 @@
     got = lax.all_to_all(
         outgoing.reshape(devices, 1, stride * depth), both, split_axis=0, concat_axis=0, tiled=True
     ).reshape(devices * stride, depth)
-    source, yfirst, ylast, density = pl.pallas_call(
-        functools.partial(owner_kernel, capacity=capacity),
+    field = filtered.reshape(width_x * width_y, depth)
+    face_y = shape((2, width_x, depth), F32)
+    values, y_hot, x_of, yeven, yodd, density = pl.pallas_call(
+        functools.partial(owner_kernel, capacity=capacity, width_y=width_y),
         out_shape=(
-            shape((width_x, width_y, depth), F32),
-            shape((2, width_x, depth), F32),
-            shape((2, width_x, depth), F32),
+            pltpu.HBM((slots, 2 * depth), BF16),
+            shape((width_y, slots), BF16),
+            shape((1, slots), I32),
+            face_y,
+            face_y,
             shape((devices, 1, capacity), F32),
         ),
+        in_specs=[smem, vmem, vmem],
+        out_specs=(hbm,) + (vmem,) * 5,
         scratch_shapes=[
+            pltpu.VMEM((slots, 2 * depth), BF16),
             pltpu.VMEM((devices, depth), F32),
             pltpu.VMEM((devices, depth), I32),
             pltpu.VMEM((slots, depth), F32),
-            pltpu.VMEM((slots, 2 * depth), BF16),
-            pltpu.VMEM((width_y, slots), BF16),
             pltpu.SMEM((devices, depth), I32),
-            pltpu.SemaphoreType.DMA,
+            pltpu.SemaphoreType.DMA((2,)),
         ],
         compiler_params=params(),
         name="owners",
-    )(got, filtered.reshape(width_x * width_y, depth))
+    )(odd, got, field)
+    planes_x = width_x + 2 * step_planes(width_x) + 4
+    wide = pltpu.VMEM((planes_x, width_y + 2 * PAD, depth), F32)
+    partial, face, xs, ys = pl.pallas_call(
+        scatter_kernel,
+        out_shape=(
+            shape(filtered.shape, F32),
+            shape((4, width_y, depth), F32),
+            shape((4, width_y, depth), F32),
+            shape((width_x, 2 * PAD, depth), F32),
+        ),
+        in_specs=[smem, hbm, vmem, vmem, hbm],
+        out_specs=(hbm, vmem, vmem, vmem),
+        scratch_shapes=[
+            pltpu.VMEM(values.shape, BF16),
+            pltpu.VMEM(field.shape, F32),
+            wide,
+            wide,
+            pltpu.VMEM((planes_x, width_y, depth), F32),
+            pltpu.SemaphoreType.DMA((width_x,)),
+        ],
+        compiler_params=params(),
+        cost_estimate=pl.CostEstimate(
+            flops=8 * slots * field.size, bytes_accessed=16 * field.size, transcendentals=field.size
+        ),
+        name="scatter",
+    )(
+        inside,
+        pltpu.with_memory_space_constraint(values, pltpu.HBM),
+        y_hot,
+        x_of,
+        pltpu.with_memory_space_constraint(field, pltpu.HBM),
+    )
 
     reply = lax.all_to_all(
         density, both, split_axis=0, concat_axis=0, tiled=True
     )
+    yeven, yodd = swap(yeven, "dom", 0), swap(yodd, "dom", 1)
+    dom_odd, brick_odd = dom % 2 == 1, brick % 2 == 1
+    ylow, yhigh = jnp.where(dom_odd, yeven, yodd), jnp.where(dom_odd, yodd, yeven)
+    filler = jnp.zeros((6, depth), F32)
+    top = jnp.concatenate([face[2], face[3], ylow[1, width_x - 1 :], yhigh[0, width_x - 1 :], filler])
+    bottom = jnp.concatenate([face[0], face[1], ylow[1, :1], yhigh[0, :1], filler])
+    top, bottom, reply = lax.optimization_barrier((top, bottom, reply))
+    xeven = swap(jnp.where(brick_odd, bottom, top), "brick", 0)
+    xodd = swap(jnp.where(brick_odd, top, bottom), "brick", 1)
     element_density = pl.pallas_call(
         reply_kernel,
         out_shape=shape((1, count), F32),
@@ -453,43 +602,16 @@
         name="reply",
     )(rank, owner_row, reply.reshape(devices, capacity))
 
-    ylow = shift(ylast, "dom", True)
-    yhigh = shift(yfirst, "dom", False)
-    top = jnp.concatenate(
-        [source[width_x - 2], source[width_x - 1], ylow[1, width_x - 1 :], yhigh[0, width_x - 1 :], jnp.zeros((6, depth), F32)]
-    )
-    bottom = jnp.concatenate(
-        [source[0], source[1], ylow[1, :1], yhigh[0, :1], jnp.zeros((6, depth), F32)]
-    )
-    from_low = shift(top, "brick", True)
-    from_high = shift(bottom, "brick", False)
-    brick, dom = lax.axis_index("brick"), lax.axis_index("dom")
-    inside = jnp.stack([brick > 0, brick < brick_count - 1, dom > 0, dom < dom_count - 1]).astype(F32)
     result = pl.pallas_call(
-        sweep_kernel,
-        out_shape=shape((width_x, width_y, depth), F32),
-        in_specs=[smem] + [vmem] * 9,
+        border_kernel,
+        out_shape=shape(filtered.shape, F32),
+        in_specs=[smem, smem, hbm] + [vmem] * 6,
         out_specs=hbm,
-        scratch_shapes=[
-            pltpu.VMEM((width_x + 4, width_y + 16, depth), F32),
-            pltpu.VMEM((width_x + 2, width_y + 16, depth), F32),
-            pltpu.VMEM((width_x, width_y, depth), F32),
-            pltpu.SemaphoreType.DMA((width_x // 8,)),
-        ],
+        scratch_shapes=[pltpu.VMEM(xs.shape, F32), pltpu.VMEM(ys.shape, F32), pltpu.SemaphoreType.DMA((4,))],
+        input_output_aliases={2: 0},
         compiler_params=params(),
-        name="sweep",
-    )(
-        inside,
-        source,
-        from_low[: 2 * width_y].reshape(2, width_y, depth),
-        from_high[: 2 * width_y].reshape(2, width_y, depth),
-        ylow,
-        yhigh,
-        yfirst[0],
-        ylast[1],
-        from_low[2 * width_y : 2 * width_y + 8],
-        from_high[2 * width_y : 2 * width_y + 8],
-    )
+        name="border",
+    )(inside, odd, partial, xs, ys, xeven, xodd, yeven, yodd)
     return (result, element_density.reshape(count))
 
 

time: 81.9 us -> 75 us (0.916)
  waiting for transfers between devices: 33.3 us -> 27.8 us
  starting transfers between devices: 21.9 us -> 18.3 us
  Pallas kernels: 23.7 us -> 26.9 us
  local copies, waits for them, and re-layouts: 1.7 us -> 0.72 us
    ppermute x4, waiting for transfers between devices: 6.55 us -> 1.08 us  [swap(): return lax.ppermute(x, axis, pairs + [(j, i) for i, j in pairs])]
    ppermute x4, starting transfers between devices: 12 us -> 8.38 us  [swap(): return lax.ppermute(x, axis, pairs + [(j, i) for i, j in pairs])]
    pallas_call x2 -> x3, Pallas kernels: 14.6 us -> 17.5 us  [the longest x1 9.89 us: body(): pl.pallas_call(scatter_kernel, out_shape=(shape(filtered.shape, F32), sha...]
    unnamed x6 -> x8, local copies, waits for them, and re-layouts: 1.6 us -> 0.64 us
  transfers between devices with their start and end apart: 6 -> 6, of which waited for: 3 -> 2; matrix products, arithmetic and copies ran while one was open for 0% -> 0% of each run, Pallas kernels for 1% -> 14%
where the time goes in v3:
time: 75 us; the launch traced here: 74.7 us
  waiting for transfers between devices  27.8 us (37%)
  Pallas kernels  26.9 us (36%)
  starting transfers between devices  18.3 us (24%)
  between operations  0.83 us (1%)
    all_to_all x1, waiting for transfers between devices, body(): lax.all_to_all(outgoing.reshape(devices, 1, stride * depth), both, split_...  26.7 us
    pallas_call x1, Pallas kernels, body(): pl.pallas_call(scatter_kernel, out_shape=(shape(filtered.shape, F32), sha...  9.89 us
    pallas_call x1, Pallas kernels, body(): pl.pallas_call(functools.partial(send_kernel, devices=devices, capacity=c...  8.64 us
    ppermute x4, starting transfers between devices, swap(): return lax.ppermute(x, axis, pairs + [(j, i) for i, j in pairs])  8.38 us
    all_to_all x1, starting transfers between devices, body(): lax.all_to_all(outgoing.reshape(devices, 1, stride * depth), both, split_...  6.42 us
    pallas_call x1, Pallas kernels, body(): pl.pallas_call(functools.partial(owner_kernel, capacity=capacity, width_y...  5.93 us
    all_to_all x1, starting transfers between devices, body(): lax.all_to_all(density, both, split_axis=0, concat_axis=0, tiled=True)  3.52 us
    pallas_call x1, Pallas kernels, body(): pl.pallas_call(border_kernel, out_shape=shape(filtered.shape, F32), in_sp...  1.68 us
  transfers between devices with their start and end apart: 6, of which 2 were waited for; matrix products, arithmetic and copies ran while one was open for 0% of the time, Pallas kernels for 14%

profile of v3, /device:TPU:5, one launch (start us, length us, event | category | flops | bytes accessed | tf_op | source)
XLA Modules:
  0.0 74.7 jit_solution(8445234533548487733)
XLA Ops:
  0.6 0.0 copy-start
  0.6 8.6 %send.1 = (f32[2080,128]{1,0:T(8,128)}, s32[1,1024]{1,0:T(1,128)}) custom-call(s32[1,1024]{1,0:T(1,128)} %bitcast.34, s32[1,1024]{1,0:T(1,128)} %bitcast.37, f32[1,1024]{1,0:T(1,128)} %bitcast.38, bf16[3,27,1024]{2,1,0:T(8,128)(2,1)} %vel_at.1, bf16[3,27,1024]{2,1,0:T(8,128)(2,1)} %adj_at.1, bf16[27,27]{1,0:T(8,128)(2,1)} %coup_at.1, s32[128,1024]{1,0:T(8,128)} %off_at.1, ...), custom_call_target="tpu_custom_call" | custom-call | tf_op jit(solution)/shard_map/send/pallas_call | solution.py:490
  9.3 6.4 %all-to-all-start = ((f32[32,1,8320]{2,1,0:T(1,128)}), f32[32,1,8320]{2,1,0:T(1,128)S(1)}, u32[]{:S(2)}, u32[]{:S(2)}) async-start(f32[32,1,8320]{2,1,0:T(1,128)} %bitcast.36), calls=%async_computation | async-start | bytes 2129920 | tf_op jit(solution)/shard_map/all_to_all | solution.py:525
  15.7 0.1 pad_add_fusion.odd_ref
  15.8 0.1 add_convert_fusion.inside_ref
  15.9 26.7 %all-to-all-done = f32[32,1,8320]{2,1,0:T(1,128)S(1)} async-done(((f32[32,1,8320]{2,1,0:T(1,128)}), f32[32,1,8320]{2,1,0:T(1,128)S(1)}, u32[]{:S(2)}, u32[]{:S(2)}) %all-to-all-start) | async-done | bytes 1064992 | tf_op jit(solution)/shard_map/all_to_all | solution.py:525
  42.6 0.0 copy-done
  42.6 5.9 %owners.1 = (bf16[2048,256]{1,0:T(8,128)(2,1)}, bf16[64,2048]{1,0:T(8,128)(2,1)S(1)}, s32[1,2048]{1,0:T(1,128)S(1)}, f32[2,64,128]{2,1,0:T(8,128)S(1)}, f32[2,64,128]{2,1,0:T(8,128)S(1)}, /*index=5*/f32[32,1,64]{2,1,0:T(1,128)}) custom-call(s32[2]{0:T(128)S(1)} %pad_add_fusion.odd_ref, f32[2080,128]{1,0:T(8,128)S(1)} %bitcast.30, f32[4096,128]{1,0:T(8,128)S(1)} %bitcast.32), custom_call_target="tpu_custom_call" | custom-call | tf_op jit(solution)/shard_map/owners/pallas_call | solution.py:530
  48.5 0.0 copy-start.3
  48.5 0.6 copy-done.3
  49.1 3.5 %all-to-all-start.1 = ((f32[32,1,64]{2,1,0:T(1,128)}), f32[32,1,64]{2,1,0:T(1,128)S(1)}, u32[]{:S(2)}, u32[]{:S(2)}) async-start(f32[32,1,64]{2,1,0:T(1,128)} %get-tuple-element.27), calls=%async_computation.1 | async-start | bytes 32768 | tf_op jit(solution)/shard_map/all_to_all | solution.py:586
  52.7 0.1 collective-permute-start
  52.8 4.3 %collective-permute-start.1 = (f32[2,64,128]{2,1,0:T(8,128)S(1)}, f32[2,64,128]{2,1,0:T(8,128)S(1)}, u32[]{:S(2)}, u32[]{:S(2)}) collective-permute-start(f32[2,64,128]{2,1,0:T(8,128)S(1)} %get-tuple-element.26), channel_id=1, source_target_pairs={{1,2},{3,4},{5,6},{2,1},{4,3},{6,5},{9,10},{11,12},{13,14},{10,9},... | collective-permute-start | bytes 196616 | tf_op jit(solution)/shard_map/ppermute | solution.py:466
  57.1 0.0 copy-start.1
  57.1 0.0 copy-start.2
  57.1 9.9 %scatter.1 = (f32[64,64,128]{2,1,0:T(8,128)}, f32[4,64,128]{2,1,0:T(8,128)S(1)}, f32[4,64,128]{2,1,0:T(8,128)S(1)}, f32[64,16,128]{2,1,0:T(8,128)S(1)}) custom-call(f32[4]{0:T(128)S(1)} %add_convert_fusion.inside_ref, bf16[2048,256]{1,0:T(8,128)(2,1)} %get-tuple-element.18.val_at, bf16[64,2048]{1,0:T(8,128)(2,1)S(1)} %get-tuple-element.19.y_ref, ...), custom_call_target="tpu_custom_call" | custom-call | flops 8589934592 | bytes 8388608 | tf_op jit(solution)/shard_map/scatter/pallas_call | solution.py:555
  67.0 0.0 collective-permute-done.yeven_ref
  67.0 0.0 collective-permute-done.1.yodd_ref
  67.1 0.0 all-to-all-done.1
  67.2 3.9 %collective-permute-start.3 = (f32[136,128]{1,0:T(8,128)S(1)}, f32[136,128]{1,0:T(8,128)S(1)}, u32[]{:S(2)}, u32[]{:S(2)}) collective-permute-start(f32[136,128]{1,0:T(8,128)S(1)} %get-tuple-element.32), channel_id=1, source_target_pairs={{8,16},{16,8},{9,17},{17,9},{10,18},{18,10},{11,19},{19,11},{12,20... | collective-permute-start | bytes 208904 | tf_op jit(solution)/shard_map/ppermute | solution.py:466
  71.1 0.1 collective-permute-start.2
  71.2 0.0 copy-done.1
  71.2 0.0 copy-done.2
  71.2 0.8 %reply.1 = f32[1,1024]{1,0:T(1,128)} custom-call(s32[1,1024]{1,0:T(1,128)S(1)} %copy-done.2, s32[1,1024]{1,0:T(1,128)S(1)} %bitcast.35, f32[32,64]{1,0:T(8,128)S(1)} %bitcast.33), custom_call_target="tpu_custom_call" | custom-call | tf_op jit(solution)/shard_map/reply/pallas_call | solution.py:598
  72.0 1.1 %collective-permute-done.3.xodd_ref = f32[136,128]{1,0:T(8,128)S(1)} collective-permute-done((f32[136,128]{1,0:T(8,128)S(1)}, f32[136,128]{1,0:T(8,128)S(1)}, u32[]{:S(2)}, u32[]{:S(2)}) %collective-permute-start.3) | collective-permute-done | bytes 69664 | tf_op jit(solution)/shard_map/ppermute | solution.py:466
  73.1 0.0 collective-permute-done.2.xeven_ref
  73.1 1.7 %border.1 = f32[64,64,128]{2,1,0:T(8,128)} custom-call(f32[4]{0:T(128)S(1)} %add_convert_fusion.inside_ref, s32[2]{0:T(128)S(1)} %pad_add_fusion.odd_ref, f32[64,64,128]{2,1,0:T(8,128)} %get-tuple-element.21.partial_at, f32[4,64,128]{2,1,0:T(8,128)S(1)} %get-tuple-element.22.xs_ref, ...), custom_call_target="tpu_custom_call", output_to_operand_aliasing={{}: (2, {})} | custom-call | tf_op jit(solution)/shard_map/border/pallas_call | solution.py:605
  (7 shorter events, 0.1 us)
Async XLA Ops:
  0.6 41.9 %copy-start = (f32[64,64,128]{2,1,0:T(8,128)S(1)}, f32[64,64,128]{2,1,0:T(8,128)}, u32[]{:S(2)}) copy-start(f32[64,64,128]{2,1,0:T(8,128)} %param.17) | copy-start | bytes 6291460
  9.3 33.3 %all-to-all-start = ((f32[32,1,8320]{2,1,0:T(1,128)}), f32[32,1,8320]{2,1,0:T(1,128)S(1)}, u32[]{:S(2)}, u32[]{:S(2)}) async-start(f32[32,1,8320]{2,1,0:T(1,128)} %bitcast.36), calls=%async_computation | async-start | bytes 2129920 | tf_op jit(solution)/shard_map/all_to_all | solution.py:525
  48.5 0.6 copy-start.3
  49.1 18.0 %all-to-all-start.1 = ((f32[32,1,64]{2,1,0:T(1,128)}), f32[32,1,64]{2,1,0:T(1,128)S(1)}, u32[]{:S(2)}, u32[]{:S(2)}) async-start(f32[32,1,64]{2,1,0:T(1,128)} %get-tuple-element.27), calls=%async_computation.1 | async-start | bytes 32768 | tf_op jit(solution)/shard_map/all_to_all | solution.py:586
  52.7 14.4 %collective-permute-start = (f32[2,64,128]{2,1,0:T(8,128)}, f32[2,64,128]{2,1,0:T(8,128)S(1)}, u32[]{:S(2)}, u32[]{:S(2)}) collective-permute-start(f32[2,64,128]{2,1,0:T(8,128)} %copy-done.3), channel_id=1, source_target_pairs={{0,1},{2,3},{4,5},{6,7},{1,0},{3,2},{5,4},{7,6},{8,9},{10,11},{12,... | collective-permute-start | bytes 196616 | tf_op jit(solution)/shard_map/ppermute | solution.py:466
  52.8 14.2 %collective-permute-start.1 = (f32[2,64,128]{2,1,0:T(8,128)S(1)}, f32[2,64,128]{2,1,0:T(8,128)S(1)}, u32[]{:S(2)}, u32[]{:S(2)}) collective-permute-start(f32[2,64,128]{2,1,0:T(8,128)S(1)} %get-tuple-element.26), channel_id=1, source_target_pairs={{1,2},{3,4},{5,6},{2,1},{4,3},{6,5},{9,10},{11,12},{13,14},{10,9},... | collective-permute-start | bytes 196616 | tf_op jit(solution)/shard_map/ppermute | solution.py:466
  57.1 14.1 %copy-start.1 = (s32[1024,1]{0,1:T(1,128)S(1)}, s32[1024,1]{0,1:T(1,128)}, u32[]{:S(2)}) copy-start(s32[1024,1]{0,1:T(1,128)} %param.13) | copy-start | bytes 12292
  57.1 14.1 %copy-start.2 = (s32[1,1024]{1,0:T(1,128)S(1)}, s32[1,1024]{1,0:T(1,128)}, u32[]{:S(2)}) copy-start(s32[1,1024]{1,0:T(1,128)} %get-tuple-element.30.rank_ref) | copy-start | bytes 12292
  67.2 5.9 %collective-permute-start.3 = (f32[136,128]{1,0:T(8,128)S(1)}, f32[136,128]{1,0:T(8,128)S(1)}, u32[]{:S(2)}, u32[]{:S(2)}) collective-permute-start(f32[136,128]{1,0:T(8,128)S(1)} %get-tuple-element.32), channel_id=1, source_target_pairs={{8,16},{16,8},{9,17},{17,9},{10,18},{18,10},{11,19},{19,11},{12,20... | collective-permute-start | bytes 208904 | tf_op jit(solution)/shard_map/ppermute | solution.py:466
  71.1 2.0 %collective-permute-start.2 = (f32[136,128]{1,0:T(8,128)S(1)}, f32[136,128]{1,0:T(8,128)S(1)}, u32[]{:S(2)}, u32[]{:S(2)}) collective-permute-start(f32[136,128]{1,0:T(8,128)S(1)} %get-tuple-element.33), channel_id=1, source_target_pairs={{0,8},{16,24},{8,0},{24,16},{1,9},{17,25},{9,1},{25,17},{2,10},{18... | collective-permute-start | bytes 208904 | tf_op jit(solution)/shard_map/ppermute | solution.py:466

commit v4 on v3

--- a/solution.py
+++ b/solution.py
@@ -119,7 +119,7 @@
     high_of = lax.broadcasted_iota(I32, (highs, entries), 0)
     low_of = lax.broadcasted_iota(I32, (lows, entries), 0)
     set_of = lax.broadcasted_iota(I32, (highs, group), 1) // lows
-    unroll = 32
+    unroll = 64
 
     def step(i, _):
         for j in range(unroll):
@@ -133,9 +133,9 @@
                 right.append(
                     (jnp.broadcast_to(low_ref[b, pl.ds(g, 1), :], (lows, entries)) == low_of).astype(F32)
                 )
-            both = dot_nt(
+            both = dot_nn(
                 jnp.concatenate(left, axis=0).astype(BF16),
-                jnp.concatenate(right, axis=0).astype(BF16),
+                jnp.concatenate(right, axis=0).T.astype(BF16),
             )
             hist = jnp.zeros((highs, group), F32)
             for b in range(sets):
@@ -186,7 +186,9 @@
     return sharpness * inverse * (1.0 - tangent * tangent)
 
 
-def owner_kernel(odd_ref, got_ref, field_ref, val_at, y_ref, x_ref, yeven_ref, yodd_ref, dens_ref, val_ref, meta_ref, block_ref, found_ref, number_ref, sems, *, capacity, width_y):
+def owner_kernel(odd_ref, got_ref, field_at, val_ref, y_ref, x_ref, yeven_ref, yodd_ref, dens_ref, meta_ref, block_ref, found_ref, number_ref, field_ref, layers_ref, sem, load_sem, *, capacity, width_y):
+    load = pltpu.make_async_copy(field_at, field_ref, load_sem)
+    load.start()
     devices = dens_ref.shape[0]
     stride = got_ref.shape[0] // devices
     depth = got_ref.shape[1]
@@ -199,7 +201,7 @@
         meta_ref[d : d + 1, :] = got_ref[row : row + 1, :]
     meta = meta_ref[...]
     block_ref[...] = meta.astype(I32)
-    copy = pltpu.make_async_copy(block_ref, number_ref, sems.at[0])
+    copy = pltpu.make_async_copy(block_ref, number_ref, sem)
     copy.start()
     prods = meta.T
     joined = group // capacity
@@ -216,7 +218,13 @@
     x_row = joint // width_y
     y_row = joint % width_y
     x_ref[...] = x_row
+    x_hot = (lax.broadcasted_iota(I32, (width_x, rows), 0) == x_row).astype(F32).astype(BF16)
+    ys = (0, 1, width_y - 2, width_y - 1)
+    for i, y in enumerate(ys):
+        at_y = jnp.broadcast_to((y_row == y).astype(F32), (width_x, rows)).astype(BF16)
+        layers_ref[i * width_x : (i + 1) * width_x, :] = x_hot * at_y
     copy.wait()
+    load.wait()
 
     def look(d, _):
         for r in range(capacity):
@@ -246,15 +254,7 @@
         val_ref[at, :depth] = high
         val_ref[at, depth:] = low
 
-    store = pltpu.make_async_copy(val_ref, val_at, sems.at[1])
-    store.start()
-
-    x_hot = (lax.broadcasted_iota(I32, (width_x, rows), 0) == x_row).astype(F32).astype(BF16)
-    ys = (0, 1, width_y - 2, width_y - 1)
-    here = [
-        x_hot * jnp.broadcast_to((y_row == y).astype(F32), (width_x, rows)).astype(BF16) for y in ys
-    ]
-    summed = dot_nn(jnp.concatenate(here, axis=0), val_ref[...])
+    summed = dot_nn(layers_ref[...], val_ref[...])
     summed = summed[:, :depth] + summed[:, depth:]
     faces = []
     for i, y in enumerate(ys):
@@ -264,7 +264,6 @@
     for i in range(2):
         yeven_ref[i] = jnp.where(odd, faces[i], faces[2 + i])
         yodd_ref[i] = jnp.where(odd, faces[2 + i], faces[i])
-    store.wait()
 
 
 def along_z(x):
@@ -310,8 +309,7 @@
     return planes
 
 
-def scatter_kernel(inside_ref, val_at, y_ref, x_ref, field_at, out_at, face_ref, xs_ref, ys_ref, val_ref, field_ref, wide_ref, near_ref, out_ref, sems):
-    loads = fetch([val_at, field_at], [val_ref, field_ref], sems)
+def scatter_kernel(inside_ref, val_ref, y_ref, x_ref, field_at, out_at, face_ref, xs_ref, ys_ref, field_ref, wide_ref, near_ref, out_ref, sems):
     rows = val_ref.shape[0]
     width_x, width_y = ys_ref.shape[0], xs_ref.shape[1]
     depth = out_ref.shape[2]
@@ -323,6 +321,13 @@
     tile = planes * width_y
     steps = width_x // planes
     lead = 2 * planes + 3
+
+    def load(i):
+        at = pl.ds(pl.multiple_of(i * tile, tile), tile)
+        return pltpu.make_async_copy(field_at.at[at], field_ref.at[at], sems.at[steps + i])
+
+    for i in range(steps):
+        load(i).start()
     for ref in (wide_ref, near_ref):
         edges = (*range(lead), lead + width_x)
         for x in edges:
@@ -360,6 +365,7 @@
         wide_ref[pl.ds(lead + i * planes, planes), inner, :] = source.reshape(planes, width_y, depth)
 
     def step(i, _):
+        load(i).wait()
         at = i * planes
         for j in range(planes):
             sweeps(lead + at - 2 * planes - 2 + j)
@@ -374,9 +380,8 @@
         pl.when(i >= 3)(done)
         return 0
 
-    loads[0].wait()
     summed = gather(0)
-    loads[1].wait()
+    load(0).wait()
     spread(0, summed)
     lax.fori_loop(1, steps, step, 0)
     for x in range((steps - 1) * planes - 1, width_x):
@@ -530,26 +535,28 @@
     values, y_hot, x_of, yeven, yodd, density = pl.pallas_call(
         functools.partial(owner_kernel, capacity=capacity, width_y=width_y),
         out_shape=(
-            pltpu.HBM((slots, 2 * depth), BF16),
+            shape((slots, 2 * depth), BF16),
             shape((width_y, slots), BF16),
             shape((1, slots), I32),
             face_y,
             face_y,
             shape((devices, 1, capacity), F32),
         ),
-        in_specs=[smem, vmem, vmem],
-        out_specs=(hbm,) + (vmem,) * 5,
+        in_specs=[smem, vmem, hbm],
+        out_specs=(vmem,) * 6,
         scratch_shapes=[
-            pltpu.VMEM((slots, 2 * depth), BF16),
             pltpu.VMEM((devices, depth), F32),
             pltpu.VMEM((devices, depth), I32),
             pltpu.VMEM((slots, depth), F32),
             pltpu.SMEM((devices, depth), I32),
-            pltpu.SemaphoreType.DMA((2,)),
+            pltpu.VMEM(field.shape, F32),
+            pltpu.VMEM((4 * width_x, slots), BF16),
+            pltpu.SemaphoreType.DMA,
+            pltpu.SemaphoreType.DMA,
         ],
         compiler_params=params(),
         name="owners",
-    )(odd, got, field)
+    )(odd, got, pltpu.with_memory_space_constraint(field, pltpu.HBM))
     planes_x = width_x + 2 * step_planes(width_x) + 4
     wide = pltpu.VMEM((planes_x, width_y + 2 * PAD, depth), F32)
     partial, face, xs, ys = pl.pallas_call(
@@ -560,28 +567,21 @@
             shape((4, width_y, depth), F32),
             shape((width_x, 2 * PAD, depth), F32),
         ),
-        in_specs=[smem, hbm, vmem, vmem, hbm],
+        in_specs=[smem, vmem, vmem, vmem, hbm],
         out_specs=(hbm, vmem, vmem, vmem),
         scratch_shapes=[
-            pltpu.VMEM(values.shape, BF16),
             pltpu.VMEM(field.shape, F32),
             wide,
             wide,
             pltpu.VMEM((planes_x, width_y, depth), F32),
-            pltpu.SemaphoreType.DMA((width_x,)),
+            pltpu.SemaphoreType.DMA((2 * width_x // step_planes(width_x),)),
         ],
         compiler_params=params(),
         cost_estimate=pl.CostEstimate(
             flops=8 * slots * field.size, bytes_accessed=16 * field.size, transcendentals=field.size
         ),
         name="scatter",
-    )(
-        inside,
-        pltpu.with_memory_space_constraint(values, pltpu.HBM),
-        y_hot,
-        x_of,
-        pltpu.with_memory_space_constraint(field, pltpu.HBM),
-    )
+    )(inside, values, y_hot, x_of, pltpu.with_memory_space_constraint(field, pltpu.HBM))
 
     reply = lax.all_to_all(
         density, both, split_axis=0, concat_axis=0, tiled=True

time: 75 us -> 71.5 us (0.953)
  Pallas kernels: 26.9 us -> 24 us
    pallas_call x1, Pallas kernels: 9.89 us -> 8.51 us  [body(): pl.pallas_call(scatter_kernel, out_shape=(shape(filtered.shape, F32), sha...]
    pallas_call x1, Pallas kernels: 8.64 us -> 7.34 us  [body(): pl.pallas_call(functools.partial(send_kernel, devices=devices, capacity=c...]
  transfers between devices with their start and end apart: 6 -> 6, of which waited for: 2 -> 2; matrix products, arithmetic and copies ran while one was open for 0% -> 0% of each run, Pallas kernels for 14% -> 13%
where the time goes in v4:
time: 71.5 us; the launch traced here: 71.2 us
  waiting for transfers between devices  27.8 us (39%)
  Pallas kernels  24 us (34%)
  starting transfers between devices  18.3 us (26%)
  between operations  0.82 us (1%)
    all_to_all x1, waiting for transfers between devices, body(): lax.all_to_all(outgoing.reshape(devices, 1, stride * depth), both, split_...  26.7 us
    pallas_call x1, Pallas kernels, body(): pl.pallas_call(scatter_kernel, out_shape=(shape(filtered.shape, F32), sha...  8.51 us
    ppermute x4, starting transfers between devices, swap(): return lax.ppermute(x, axis, pairs + [(j, i) for i, j in pairs])  8.38 us
    pallas_call x1, Pallas kernels, body(): pl.pallas_call(functools.partial(send_kernel, devices=devices, capacity=c...  7.34 us
    all_to_all x1, starting transfers between devices, body(): lax.all_to_all(outgoing.reshape(devices, 1, stride * depth), both, split_...  6.42 us
    pallas_call x1, Pallas kernels, body(): pl.pallas_call(functools.partial(owner_kernel, capacity=capacity, width_y...  5.69 us
    all_to_all x1, starting transfers between devices, body(): lax.all_to_all(density, both, split_axis=0, concat_axis=0, tiled=True)  3.49 us
    pallas_call x1, Pallas kernels, body(): pl.pallas_call(border_kernel, out_shape=shape(filtered.shape, F32), in_sp...  1.69 us
  transfers between devices with their start and end apart: 6, of which 2 were waited for; matrix products, arithmetic and copies ran while one was open for 0% of the time, Pallas kernels for 13%

profile of v4, /device:TPU:5, one launch (start us, length us, event | category | flops | bytes accessed | tf_op | source)
XLA Modules:
  0.0 71.2 jit_solution(13693186585044633737)
XLA Ops:
  0.6 7.3 %send.1 = (f32[2080,128]{1,0:T(8,128)}, s32[1,1024]{1,0:T(1,128)}) custom-call(s32[1,1024]{1,0:T(1,128)} %bitcast.32, s32[1,1024]{1,0:T(1,128)} %bitcast.37, f32[1,1024]{1,0:T(1,128)} %bitcast.38, bf16[3,27,1024]{2,1,0:T(8,128)(2,1)} %vel_at.1, bf16[3,27,1024]{2,1,0:T(8,128)(2,1)} %adj_at.1, bf16[27,27]{1,0:T(8,128)(2,1)} %coup_at.1, s32[128,1024]{1,0:T(8,128)} %off_at.1, ...), custom_call_target="tpu_custom_call" | custom-call | tf_op jit(solution)/shard_map/send/pallas_call | solution.py:495
  8.0 6.4 %all-to-all-start = ((f32[32,1,8320]{2,1,0:T(1,128)}), f32[32,1,8320]{2,1,0:T(1,128)S(1)}, u32[]{:S(2)}, u32[]{:S(2)}) async-start(f32[32,1,8320]{2,1,0:T(1,128)} %bitcast.36), calls=%async_computation | async-start | bytes 2129920 | tf_op jit(solution)/shard_map/all_to_all | solution.py:530
  14.4 0.1 pad_add_fusion.odd_ref
  14.5 0.1 add_convert_fusion.inside_ref
  14.6 26.7 %all-to-all-done = f32[32,1,8320]{2,1,0:T(1,128)S(1)} async-done(((f32[32,1,8320]{2,1,0:T(1,128)}), f32[32,1,8320]{2,1,0:T(1,128)S(1)}, u32[]{:S(2)}, u32[]{:S(2)}) %all-to-all-start) | async-done | bytes 1064992 | tf_op jit(solution)/shard_map/all_to_all | solution.py:530
  41.3 5.7 %owners.1 = (bf16[2048,256]{1,0:T(8,128)(2,1)S(1)}, bf16[64,2048]{1,0:T(8,128)(2,1)S(1)}, s32[1,2048]{1,0:T(1,128)S(1)}, f32[2,64,128]{2,1,0:T(8,128)S(1)}, f32[...) custom-call(s32[2]{0:T(128)S(1)} %pad_add_fusion.odd_ref, f32[2080,128]{1,0:T(8,128)S(1)} %bitcast.30, f32[4096,128]{1,0:T(8,128)} %bitcast.34), custom_call_target="tpu_custom_call" | custom-call | tf_op jit(solution)/shard_map/owners/pallas_call | solution.py:535
  47.0 3.5 %all-to-all-start.1 = ((f32[32,1,64]{2,1,0:T(1,128)}), f32[32,1,64]{2,1,0:T(1,128)S(1)}, u32[]{:S(2)}, u32[]{:S(2)}) async-start(f32[32,1,64]{2,1,0:T(1,128)} %get-tuple-element.27), calls=%async_computation.1 | async-start | bytes 32768 | tf_op jit(solution)/shard_map/all_to_all | solution.py:586
  50.5 0.1 collective-permute-start
  50.6 4.3 %collective-permute-start.1 = (f32[2,64,128]{2,1,0:T(8,128)S(1)}, f32[2,64,128]{2,1,0:T(8,128)S(1)}, u32[]{:S(2)}, u32[]{:S(2)}) collective-permute-start(f32[2,64,128]{2,1,0:T(8,128)S(1)} %get-tuple-element.26), channel_id=1, source_target_pairs={{1,2},{3,4},{5,6},{2,1},{4,3},{6,5},{9,10},{11,12},{13,14},{10,9},... | collective-permute-start | bytes 196616 | tf_op jit(solution)/shard_map/ppermute | solution.py:471
  54.9 0.0 copy-start
  54.9 0.0 copy-start.1
  54.9 8.5 %scatter.1 = (f32[64,64,128]{2,1,0:T(8,128)}, f32[4,64,128]{2,1,0:T(8,128)S(1)}, f32[4,64,128]{2,1,0:T(8,128)S(1)}, f32[64,16,128]{2,1,0:T(8,128)S(1)}) custom-call(f32[4]{0:T(128)S(1)} %add_convert_fusion.inside_ref, bf16[2048,256]{1,0:T(8,128)(2,1)S(1)} %get-tuple-element.18.val_ref, bf16[64,2048]{1,0:T(8,128)(2,1)S(1)} %get-tuple-element.19.y_ref, ...), custom_call_target="tpu_custom_call" | custom-call | flops 8589934592 | bytes 8388608 | tf_op jit(solution)/shard_map/scatter/pallas_call | solution.py:562
  63.4 0.0 collective-permute-done.yeven_ref
  63.4 0.0 collective-permute-done.1.yodd_ref
  63.5 0.0 all-to-all-done.1
  63.6 3.9 %collective-permute-start.3 = (f32[136,128]{1,0:T(8,128)S(1)}, f32[136,128]{1,0:T(8,128)S(1)}, u32[]{:S(2)}, u32[]{:S(2)}) collective-permute-start(f32[136,128]{1,0:T(8,128)S(1)} %get-tuple-element.32), channel_id=1, source_target_pairs={{8,16},{16,8},{9,17},{17,9},{10,18},{18,10},{11,19},{19,11},{12,20... | collective-permute-start | bytes 208904 | tf_op jit(solution)/shard_map/ppermute | solution.py:471
  67.5 0.1 collective-permute-start.2
  67.6 0.0 copy-done
  67.6 0.0 copy-done.1
  67.6 0.8 %reply.1 = f32[1,1024]{1,0:T(1,128)} custom-call(s32[1,1024]{1,0:T(1,128)S(1)} %copy-done.1, s32[1,1024]{1,0:T(1,128)S(1)} %bitcast.33, f32[32,64]{1,0:T(8,128)S(1)} %bitcast.31), custom_call_target="tpu_custom_call" | custom-call | tf_op jit(solution)/shard_map/reply/pallas_call | solution.py:598
  68.4 1.1 %collective-permute-done.3.xodd_ref = f32[136,128]{1,0:T(8,128)S(1)} collective-permute-done((f32[136,128]{1,0:T(8,128)S(1)}, f32[136,128]{1,0:T(8,128)S(1)}, u32[]{:S(2)}, u32[]{:S(2)}) %collective-permute-start.3) | collective-permute-done | bytes 69664 | tf_op jit(solution)/shard_map/ppermute | solution.py:471
  69.5 0.0 collective-permute-done.2.xeven_ref
  69.5 1.7 %border.1 = f32[64,64,128]{2,1,0:T(8,128)} custom-call(f32[4]{0:T(128)S(1)} %add_convert_fusion.inside_ref, s32[2]{0:T(128)S(1)} %pad_add_fusion.odd_ref, f32[64,64,128]{2,1,0:T(8,128)} %get-tuple-element.21.partial_at, f32[4,64,128]{2,1,0:T(8,128)S(1)} %get-tuple-element.22.xs_ref, ...), custom_call_target="tpu_custom_call", output_to_operand_aliasing={{}: (2, {})} | custom-call | tf_op jit(solution)/shard_map/border/pallas_call | solution.py:605
  (7 shorter events, 0.1 us)
Async XLA Ops:
  8.0 33.3 %all-to-all-start = ((f32[32,1,8320]{2,1,0:T(1,128)}), f32[32,1,8320]{2,1,0:T(1,128)S(1)}, u32[]{:S(2)}, u32[]{:S(2)}) async-start(f32[32,1,8320]{2,1,0:T(1,128)} %bitcast.36), calls=%async_computation | async-start | bytes 2129920 | tf_op jit(solution)/shard_map/all_to_all | solution.py:530
  47.0 16.6 %all-to-all-start.1 = ((f32[32,1,64]{2,1,0:T(1,128)}), f32[32,1,64]{2,1,0:T(1,128)S(1)}, u32[]{:S(2)}, u32[]{:S(2)}) async-start(f32[32,1,64]{2,1,0:T(1,128)} %get-tuple-element.27), calls=%async_computation.1 | async-start | bytes 32768 | tf_op jit(solution)/shard_map/all_to_all | solution.py:586
  50.5 13.0 %collective-permute-start = (f32[2,64,128]{2,1,0:T(8,128)S(1)}, f32[2,64,128]{2,1,0:T(8,128)S(1)}, u32[]{:S(2)}, u32[]{:S(2)}) collective-permute-start(f32[2,64,128]{2,1,0:T(8,128)S(1)} %get-tuple-element.25), channel_id=1, source_target_pairs={{0,1},{2,3},{4,5},{6,7},{1,0},{3,2},{5,4},{7,6},{8,9},{10,11},{12,... | collective-permute-start | bytes 196616 | tf_op jit(solution)/shard_map/ppermute | solution.py:471
  50.6 12.9 %collective-permute-start.1 = (f32[2,64,128]{2,1,0:T(8,128)S(1)}, f32[2,64,128]{2,1,0:T(8,128)S(1)}, u32[]{:S(2)}, u32[]{:S(2)}) collective-permute-start(f32[2,64,128]{2,1,0:T(8,128)S(1)} %get-tuple-element.26), channel_id=1, source_target_pairs={{1,2},{3,4},{5,6},{2,1},{4,3},{6,5},{9,10},{11,12},{13,14},{10,9},... | collective-permute-start | bytes 196616 | tf_op jit(solution)/shard_map/ppermute | solution.py:471
  54.9 12.7 %copy-start = (s32[1024,1]{0,1:T(1,128)S(1)}, s32[1024,1]{0,1:T(1,128)}, u32[]{:S(2)}) copy-start(s32[1024,1]{0,1:T(1,128)} %param.13) | copy-start | bytes 12292
  54.9 12.7 %copy-start.1 = (s32[1,1024]{1,0:T(1,128)S(1)}, s32[1,1024]{1,0:T(1,128)}, u32[]{:S(2)}) copy-start(s32[1,1024]{1,0:T(1,128)} %get-tuple-element.30.rank_ref) | copy-start | bytes 12292
  63.6 5.9 %collective-permute-start.3 = (f32[136,128]{1,0:T(8,128)S(1)}, f32[136,128]{1,0:T(8,128)S(1)}, u32[]{:S(2)}, u32[]{:S(2)}) collective-permute-start(f32[136,128]{1,0:T(8,128)S(1)} %get-tuple-element.32), channel_id=1, source_target_pairs={{8,16},{16,8},{9,17},{17,9},{10,18},{18,10},{11,19},{19,11},{12,20... | collective-permute-start | bytes 208904 | tf_op jit(solution)/shard_map/ppermute | solution.py:471
  67.5 2.0 %collective-permute-start.2 = (f32[136,128]{1,0:T(8,128)S(1)}, f32[136,128]{1,0:T(8,128)S(1)}, u32[]{:S(2)}, u32[]{:S(2)}) collective-permute-start(f32[136,128]{1,0:T(8,128)S(1)} %get-tuple-element.33), channel_id=1, source_target_pairs={{0,8},{16,24},{8,0},{24,16},{1,9},{17,25},{9,1},{25,17},{2,10},{18... | collective-permute-start | bytes 208904 | tf_op jit(solution)/shard_map/ppermute | solution.py:471

commit v5 on v4

--- a/solution.py
+++ b/solution.py
@@ -52,7 +52,7 @@
     return copies
 
 
-def send_kernel(owner_at, block_at, jac_at, vel_at, adj_at, coup_at, off_at, mar_at, out_at, rank_ref, owner_ref, block_ref, jac_ref, vel_ref, adj_ref, coup_ref, off_ref, mar_ref, high_ref, low_ref, first_ref, second_ref, hist_ref, map_ref, out_ref, sems, *, devices, capacity):
+def send_kernel(owner_at, block_at, jac_at, vel_at, adj_at, coup_at, off_at, mar_at, out_ref, rank_ref, owner_ref, block_ref, jac_ref, vel_ref, adj_ref, coup_ref, off_ref, mar_ref, high_ref, low_ref, first_ref, second_ref, hist_ref, map_ref, sems, *, devices, capacity):
     copies = fetch(
         [owner_at, block_at, jac_at, vel_at, adj_at, coup_at, off_at, mar_at],
         [owner_ref, block_ref, jac_ref, vel_ref, adj_ref, coup_ref, off_ref, mar_ref],
@@ -157,7 +157,6 @@
 
     place = owner * stride + rank
     tile = slots // 4
-    stores = []
     for at in range(0, slots, tile):
         row_of = lax.broadcasted_iota(I32, (tile, count), 0) + at
         here = (row_of == place).astype(F32).astype(BF16)
@@ -167,13 +166,6 @@
             row = d * stride + capacity
             if at <= row < at + tile:
                 out_ref[row : row + 1, :] = meta[d : d + 1, :]
-        store = pltpu.make_async_copy(
-            out_ref.at[pl.ds(at, tile)], out_at.at[pl.ds(at, tile)], sems.at[at // tile]
-        )
-        store.start()
-        stores.append(store)
-    for store in stores:
-        store.wait()
 
 
 def constants():
@@ -186,9 +178,7 @@
     return sharpness * inverse * (1.0 - tangent * tangent)
 
 
-def owner_kernel(odd_ref, got_ref, field_at, val_ref, y_ref, x_ref, yeven_ref, yodd_ref, dens_ref, meta_ref, block_ref, found_ref, number_ref, field_ref, layers_ref, sem, load_sem, *, capacity, width_y):
-    load = pltpu.make_async_copy(field_at, field_ref, load_sem)
-    load.start()
+def owner_kernel(odd_ref, number_ref, got_ref, field_ref, given_ref, index_ref, yeven_ref, yodd_ref, dens_ref, meta_ref, block_ref, found_ref, val_ref, layers_ref, *, capacity, width_y):
     devices = dens_ref.shape[0]
     stride = got_ref.shape[0] // devices
     depth = got_ref.shape[1]
@@ -201,8 +191,6 @@
         meta_ref[d : d + 1, :] = got_ref[row : row + 1, :]
     meta = meta_ref[...]
     block_ref[...] = meta.astype(I32)
-    copy = pltpu.make_async_copy(block_ref, number_ref, sem)
-    copy.start()
     prods = meta.T
     joined = group // capacity
     index = [
@@ -211,20 +199,15 @@
         )
         for d in range(0, devices, joined)
     ]
-    y_of = lax.broadcasted_iota(I32, (width_y, group), 0)
-    for k, part in enumerate(index):
-        y_ref[:, k * group : (k + 1) * group] = (y_of == part % width_y).astype(F32).astype(BF16)
     joint = jnp.concatenate(index, axis=1)
     x_row = joint // width_y
     y_row = joint % width_y
-    x_ref[...] = x_row
+    index_ref[...] = joint
     x_hot = (lax.broadcasted_iota(I32, (width_x, rows), 0) == x_row).astype(F32).astype(BF16)
     ys = (0, 1, width_y - 2, width_y - 1)
     for i, y in enumerate(ys):
         at_y = jnp.broadcast_to((y_row == y).astype(F32), (width_x, rows)).astype(BF16)
         layers_ref[i * width_x : (i + 1) * width_x, :] = x_hot * at_y
-    copy.wait()
-    load.wait()
 
     def look(d, _):
         for r in range(capacity):
@@ -250,7 +233,9 @@
         dens_ref[d, :, :] = jnp.sum(jnp.where(diagonal, density, 0.0), axis=0, keepdims=True)[:, :capacity]
         shifted = ramp_q + density
         term = -ramp_q * (1.0 + ramp_q) / (shifted * shifted) * prods[capacity : 2 * capacity, d : d + 1]
-        high, low = parts(term * got_ref[d * stride : d * stride + capacity, :], 2)
+        value = term * got_ref[d * stride : d * stride + capacity, :]
+        given_ref[d * stride : d * stride + capacity, :] = value
+        high, low = parts(value, 2)
         val_ref[at, :depth] = high
         val_ref[at, depth:] = low
 
@@ -309,7 +294,7 @@
     return planes
 
 
-def scatter_kernel(inside_ref, val_ref, y_ref, x_ref, field_at, out_at, face_ref, xs_ref, ys_ref, field_ref, wide_ref, near_ref, out_ref, sems):
+def scatter_kernel(inside_ref, given_ref, index_ref, field_at, out_at, face_ref, xs_ref, ys_ref, val_ref, y_ref, field_ref, wide_ref, near_ref, out_ref, sems, *, capacity):
     rows = val_ref.shape[0]
     width_x, width_y = ys_ref.shape[0], xs_ref.shape[1]
     depth = out_ref.shape[2]
@@ -328,6 +313,16 @@
 
     for i in range(steps):
         load(i).start()
+    stride = given_ref.shape[0] * capacity // rows
+    for d in range(rows // capacity):
+        at = slice(d * capacity, (d + 1) * capacity)
+        high, low = parts(given_ref[d * stride : d * stride + capacity, :], 2)
+        val_ref[at, :depth] = high
+        val_ref[at, depth:] = low
+    joint = index_ref[...]
+    y_row = jnp.broadcast_to(joint % width_y, (width_y, rows))
+    y_ref[...] = (lax.broadcasted_iota(I32, (width_y, rows), 0) == y_row).astype(F32).astype(BF16)
+    x_row = joint // width_y
     for ref in (wide_ref, near_ref):
         edges = (*range(lead), lead + width_x)
         for x in edges:
@@ -354,7 +349,7 @@
         at = i * planes
         here = []
         for j in range(planes):
-            at_x = (x_ref[...] == at + j).astype(F32)
+            at_x = (x_row == at + j).astype(F32)
             here.append(y_ref[...] * jnp.broadcast_to(at_x, (width_y, rows)).astype(BF16))
         summed = dot_nn(jnp.concatenate(here, axis=0), val_ref[...])
         return summed[:, :depth] + summed[:, depth:]
@@ -496,7 +491,7 @@
         functools.partial(send_kernel, devices=devices, capacity=capacity),
         out_shape=(shape((devices * stride, depth), F32), shape((1, count), I32)),
         in_specs=[hbm] * 8,
-        out_specs=(hbm, vmem),
+        out_specs=(vmem, vmem),
         scratch_shapes=[
             pltpu.VMEM((1, count), I32),
             pltpu.VMEM((1, count), I32),
@@ -512,7 +507,6 @@
             pltpu.VMEM(turned, F32),
             pltpu.VMEM((count * depth // lanes, lanes), F32),
             pltpu.VMEM((2 * depth, count), BF16),
-            pltpu.VMEM((devices * stride, depth), F32),
             pltpu.SemaphoreType.DMA((8,)),
         ],
         compiler_params=params(VMEM_WHOLE),
@@ -532,44 +526,43 @@
     ).reshape(devices * stride, depth)
     field = filtered.reshape(width_x * width_y, depth)
     face_y = shape((2, width_x, depth), F32)
-    values, y_hot, x_of, yeven, yodd, density = pl.pallas_call(
+    values, index, yeven, yodd, density = pl.pallas_call(
         functools.partial(owner_kernel, capacity=capacity, width_y=width_y),
         out_shape=(
-            shape((slots, 2 * depth), BF16),
-            shape((width_y, slots), BF16),
+            shape(got.shape, F32),
             shape((1, slots), I32),
             face_y,
             face_y,
             shape((devices, 1, capacity), F32),
         ),
-        in_specs=[smem, vmem, hbm],
-        out_specs=(vmem,) * 6,
+        in_specs=[smem, smem, vmem, vmem],
+        out_specs=(vmem,) * 5,
+        input_output_aliases={2: 0},
         scratch_shapes=[
             pltpu.VMEM((devices, depth), F32),
             pltpu.VMEM((devices, depth), I32),
             pltpu.VMEM((slots, depth), F32),
-            pltpu.SMEM((devices, depth), I32),
-            pltpu.VMEM(field.shape, F32),
+            pltpu.VMEM((slots, 2 * depth), BF16),
             pltpu.VMEM((4 * width_x, slots), BF16),
-            pltpu.SemaphoreType.DMA,
-            pltpu.SemaphoreType.DMA,
         ],
         compiler_params=params(),
         name="owners",
-    )(odd, got, pltpu.with_memory_space_constraint(field, pltpu.HBM))
+    )(odd, got[capacity::stride].astype(I32), got, field)
     planes_x = width_x + 2 * step_planes(width_x) + 4
     wide = pltpu.VMEM((planes_x, width_y + 2 * PAD, depth), F32)
     partial, face, xs, ys = pl.pallas_call(
-        scatter_kernel,
+        functools.partial(scatter_kernel, capacity=capacity),
         out_shape=(
             shape(filtered.shape, F32),
             shape((4, width_y, depth), F32),
             shape((4, width_y, depth), F32),
             shape((width_x, 2 * PAD, depth), F32),
         ),
-        in_specs=[smem, vmem, vmem, vmem, hbm],
+        in_specs=[smem, vmem, vmem, hbm],
         out_specs=(hbm, vmem, vmem, vmem),
         scratch_shapes=[
+            pltpu.VMEM((slots, 2 * depth), BF16),
+            pltpu.VMEM((width_y, slots), BF16),
             pltpu.VMEM(field.shape, F32),
             wide,
             wide,
@@ -581,7 +574,7 @@
             flops=8 * slots * field.size, bytes_accessed=16 * field.size, transcendentals=field.size
         ),
         name="scatter",
-    )(inside, values, y_hot, x_of, pltpu.with_memory_space_constraint(field, pltpu.HBM))
+    )(inside, values, index, pltpu.with_memory_space_constraint(field, pltpu.HBM))
 
     reply = lax.all_to_all(
         density, both, split_axis=0, concat_axis=0, tiled=True

time: 71.5 us -> 70.8 us (level)
    pallas_call x1, Pallas kernels: 5.69 us -> 4.9 us  [body(): pl.pallas_call(functools.partial(owner_kernel, capacity=capacity, width_y...]
  transfers between devices with their start and end apart: 6 -> 6, of which waited for: 2 -> 2; matrix products, arithmetic and copies ran while one was open for 0% -> 0% of each run, Pallas kernels for 13% -> 14%
where the time goes in v5:
time: 70.8 us; the launch traced here: 70.6 us
  waiting for transfers between devices  27.8 us (39%)
  Pallas kernels  23.5 us (33%)
  starting transfers between devices  18.2 us (26%)
  between operations  0.83 us (1%)
    all_to_all x1, waiting for transfers between devices, body(): lax.all_to_all(outgoing.reshape(devices, 1, stride * depth), both, split_...  26.7 us
    pallas_call x1, Pallas kernels, body(): pl.pallas_call(functools.partial(scatter_kernel, capacity=capacity), out_...  9.01 us
    ppermute x4, starting transfers between devices, swap(): return lax.ppermute(x, axis, pairs + [(j, i) for i, j in pairs])  8.38 us
    pallas_call x1, Pallas kernels, body(): pl.pallas_call(functools.partial(send_kernel, devices=devices, capacity=c...  7.07 us
    all_to_all x1, starting transfers between devices, body(): lax.all_to_all(outgoing.reshape(devices, 1, stride * depth), both, split_...  6.41 us
    pallas_call x1, Pallas kernels, body(): pl.pallas_call(functools.partial(owner_kernel, capacity=capacity, width_y...  4.9 us
    all_to_all x1, starting transfers between devices, body(): lax.all_to_all(density, both, split_axis=0, concat_axis=0, tiled=True)  3.43 us
    pallas_call x1, Pallas kernels, body(): pl.pallas_call(border_kernel, out_shape=shape(filtered.shape, F32), in_sp...  1.68 us
  transfers between devices with their start and end apart: 6, of which 2 were waited for; matrix products, arithmetic and copies ran while one was open for 0% of the time, Pallas kernels for 14%

profile of v5, /device:TPU:5, one launch (start us, length us, event | category | flops | bytes accessed | tf_op | source)
XLA Modules:
  0.0 70.6 jit_solution(9408708647055999096)
XLA Ops:
  0.6 0.0 copy-start
  0.6 7.1 %send.1 = (f32[2080,128]{1,0:T(8,128)}, s32[1,1024]{1,0:T(1,128)}) custom-call(s32[1,1024]{1,0:T(1,128)} %bitcast.35, s32[1,1024]{1,0:T(1,128)} %bitcast.38, f32[1,1024]{1,0:T(1,128)} %bitcast.39, bf16[3,27,1024]{2,1,0:T(8,128)(2,1)} %vel_at.1, bf16[3,27,1024]{2,1,0:T(8,128)(2,1)} %adj_at.1, bf16[27,27]{1,0:T(8,128)(2,1)} %coup_at.1, s32[128,1024]{1,0:T(8,128)} %off_at.1, ...), custom_call_target="tpu_custom_call" | custom-call | tf_op jit(solution)/shard_map/send/pallas_call | solution.py:490
  7.7 6.4 %all-to-all-start = ((f32[32,1,8320]{2,1,0:T(1,128)}), f32[32,1,8320]{2,1,0:T(1,128)S(1)}, u32[]{:S(2)}, u32[]{:S(2)}) async-start(f32[32,1,8320]{2,1,0:T(1,128)} %bitcast.37), calls=%async_computation | async-start | bytes 2129920 | tf_op jit(solution)/shard_map/all_to_all | solution.py:524
  14.2 0.1 pad_add_fusion.odd_ref
  14.2 0.1 add_convert_fusion.inside_ref
  14.3 26.7 %all-to-all-done = f32[32,1,8320]{2,1,0:T(1,128)S(1)} async-done(((f32[32,1,8320]{2,1,0:T(1,128)}), f32[32,1,8320]{2,1,0:T(1,128)S(1)}, u32[]{:S(2)}, u32[]{:S(2)}) %all-to-all-start) | async-done | bytes 1064992 | tf_op jit(solution)/shard_map/all_to_all | solution.py:524
  41.0 0.0 copy-done
  41.0 4.9 %owners.1 = (f32[2080,128]{1,0:T(8,128)S(1)}, s32[1,2048]{1,0:T(1,128)S(1)}, f32[2,64,128]{2,1,0:T(8,128)S(1)}, f32[2,64,128]{2,1,0:T(8,128)S(1)}, f32[32,1,64]{2,1,0:T(1,128)}) custom-call(s32[2]{0:T(128)S(1)} %pad_add_fusion.odd_ref, s32[32,128]{1,0:T(8,128)S(1)} %convert_element_type.7.number_ref, ...), custom_call_target="tpu_custom_call", output_to_operand_aliasing={{0}: (2, {})} | custom-call | tf_op jit(solution)/shard_map/owners/pallas_call | solution.py:529
  45.9 3.4 %all-to-all-start.1 = ((f32[32,1,64]{2,1,0:T(1,128)}), f32[32,1,64]{2,1,0:T(1,128)S(1)}, u32[]{:S(2)}, u32[]{:S(2)}) async-start(f32[32,1,64]{2,1,0:T(1,128)} %get-tuple-element.25), calls=%async_computation.1 | async-start | bytes 32768 | tf_op jit(solution)/shard_map/all_to_all | solution.py:579
  49.4 0.1 collective-permute-start
  49.5 4.3 %collective-permute-start.1 = (f32[2,64,128]{2,1,0:T(8,128)S(1)}, f32[2,64,128]{2,1,0:T(8,128)S(1)}, u32[]{:S(2)}, u32[]{:S(2)}) collective-permute-start(f32[2,64,128]{2,1,0:T(8,128)S(1)} %get-tuple-element.24), channel_id=1, source_target_pairs={{1,2},{3,4},{5,6},{2,1},{4,3},{6,5},{9,10},{11,12},{13,14},{10,9},... | collective-permute-start | bytes 196616 | tf_op jit(solution)/shard_map/ppermute | solution.py:466
  53.8 0.0 copy-start.1
  53.8 0.0 copy-start.2
  53.8 9.0 %scatter.1 = (f32[64,64,128]{2,1,0:T(8,128)}, f32[4,64,128]{2,1,0:T(8,128)S(1)}, f32[4,64,128]{2,1,0:T(8,128)S(1)}, f32[64,16,128]{2,1,0:T(8,128)S(1)}) custom-call(f32[4]{0:T(128)S(1)} %add_convert_fusion.inside_ref, f32[2080,128]{1,0:T(8,128)S(1)} %get-tuple-element.17.given_ref, s32[1,2048]{1,0:T(1,128)S(1)} %get-tuple-element.18.index_ref, ...), custom_call_target="tpu_custom_call" | custom-call | flops 8589934592 | bytes 8388608 | tf_op jit(solution)/shard_map/scatter/pallas_call | solution.py:553
  62.8 0.0 collective-permute-done.yeven_ref
  62.8 0.0 collective-permute-done.1.yodd_ref
  63.0 0.0 all-to-all-done.1
  63.0 3.9 %collective-permute-start.3 = (f32[136,128]{1,0:T(8,128)S(1)}, f32[136,128]{1,0:T(8,128)S(1)}, u32[]{:S(2)}, u32[]{:S(2)}) collective-permute-start(f32[136,128]{1,0:T(8,128)S(1)} %get-tuple-element.30), channel_id=1, source_target_pairs={{8,16},{16,8},{9,17},{17,9},{10,18},{18,10},{11,19},{19,11},{12,20... | collective-permute-start | bytes 208904 | tf_op jit(solution)/shard_map/ppermute | solution.py:466
  66.9 0.1 collective-permute-start.2
  67.0 0.0 copy-done.1
  67.0 0.0 copy-done.2
  67.0 0.8 %reply.1 = f32[1,1024]{1,0:T(1,128)} custom-call(s32[1,1024]{1,0:T(1,128)S(1)} %copy-done.2, s32[1,1024]{1,0:T(1,128)S(1)} %bitcast.36, f32[32,64]{1,0:T(8,128)S(1)} %bitcast.34), custom_call_target="tpu_custom_call" | custom-call | tf_op jit(solution)/shard_map/reply/pallas_call | solution.py:591
  67.8 1.1 %collective-permute-done.3.xodd_ref = f32[136,128]{1,0:T(8,128)S(1)} collective-permute-done((f32[136,128]{1,0:T(8,128)S(1)}, f32[136,128]{1,0:T(8,128)S(1)}, u32[]{:S(2)}, u32[]{:S(2)}) %collective-permute-start.3) | collective-permute-done | bytes 69664 | tf_op jit(solution)/shard_map/ppermute | solution.py:466
  68.9 0.0 collective-permute-done.2.xeven_ref
  68.9 1.7 %border.1 = f32[64,64,128]{2,1,0:T(8,128)} custom-call(f32[4]{0:T(128)S(1)} %add_convert_fusion.inside_ref, s32[2]{0:T(128)S(1)} %pad_add_fusion.odd_ref, f32[64,64,128]{2,1,0:T(8,128)} %get-tuple-element.19.partial_at, f32[4,64,128]{2,1,0:T(8,128)S(1)} %get-tuple-element.20.xs_ref, ...), custom_call_target="tpu_custom_call", output_to_operand_aliasing={{}: (2, {})} | custom-call | tf_op jit(solution)/shard_map/border/pallas_call | solution.py:598
  (9 shorter events, 0.1 us)
Async XLA Ops:
  0.6 40.4 %copy-start = (f32[64,64,128]{2,1,0:T(8,128)S(1)}, f32[64,64,128]{2,1,0:T(8,128)}, u32[]{:S(2)}) copy-start(f32[64,64,128]{2,1,0:T(8,128)} %param.17) | copy-start | bytes 6291460
  7.7 33.3 %all-to-all-start = ((f32[32,1,8320]{2,1,0:T(1,128)}), f32[32,1,8320]{2,1,0:T(1,128)S(1)}, u32[]{:S(2)}, u32[]{:S(2)}) async-start(f32[32,1,8320]{2,1,0:T(1,128)} %bitcast.37), calls=%async_computation | async-start | bytes 2129920 | tf_op jit(solution)/shard_map/all_to_all | solution.py:524
  45.9 17.0 %all-to-all-start.1 = ((f32[32,1,64]{2,1,0:T(1,128)}), f32[32,1,64]{2,1,0:T(1,128)S(1)}, u32[]{:S(2)}, u32[]{:S(2)}) async-start(f32[32,1,64]{2,1,0:T(1,128)} %get-tuple-element.25), calls=%async_computation.1 | async-start | bytes 32768 | tf_op jit(solution)/shard_map/all_to_all | solution.py:579
  49.4 13.5 %collective-permute-start = (f32[2,64,128]{2,1,0:T(8,128)S(1)}, f32[2,64,128]{2,1,0:T(8,128)S(1)}, u32[]{:S(2)}, u32[]{:S(2)}) collective-permute-start(f32[2,64,128]{2,1,0:T(8,128)S(1)} %get-tuple-element.23), channel_id=1, source_target_pairs={{0,1},{2,3},{4,5},{6,7},{1,0},{3,2},{5,4},{7,6},{8,9},{10,11},{12,... | collective-permute-start | bytes 196616 | tf_op jit(solution)/shard_map/ppermute | solution.py:466
  49.5 13.4 %collective-permute-start.1 = (f32[2,64,128]{2,1,0:T(8,128)S(1)}, f32[2,64,128]{2,1,0:T(8,128)S(1)}, u32[]{:S(2)}, u32[]{:S(2)}) collective-permute-start(f32[2,64,128]{2,1,0:T(8,128)S(1)} %get-tuple-element.24), channel_id=1, source_target_pairs={{1,2},{3,4},{5,6},{2,1},{4,3},{6,5},{9,10},{11,12},{13,14},{10,9},... | collective-permute-start | bytes 196616 | tf_op jit(solution)/shard_map/ppermute | solution.py:466
  53.8 13.2 %copy-start.1 = (s32[1024,1]{0,1:T(1,128)S(1)}, s32[1024,1]{0,1:T(1,128)}, u32[]{:S(2)}) copy-start(s32[1024,1]{0,1:T(1,128)} %param.13) | copy-start | bytes 12292
  53.8 13.2 %copy-start.2 = (s32[1,1024]{1,0:T(1,128)S(1)}, s32[1,1024]{1,0:T(1,128)}, u32[]{:S(2)}) copy-start(s32[1,1024]{1,0:T(1,128)} %get-tuple-element.28.rank_ref) | copy-start | bytes 12292
  63.0 5.9 %collective-permute-start.3 = (f32[136,128]{1,0:T(8,128)S(1)}, f32[136,128]{1,0:T(8,128)S(1)}, u32[]{:S(2)}, u32[]{:S(2)}) collective-permute-start(f32[136,128]{1,0:T(8,128)S(1)} %get-tuple-element.30), channel_id=1, source_target_pairs={{8,16},{16,8},{9,17},{17,9},{10,18},{18,10},{11,19},{19,11},{12,20... | collective-permute-start | bytes 208904 | tf_op jit(solution)/shard_map/ppermute | solution.py:466
  66.9 2.0 %collective-permute-start.2 = (f32[136,128]{1,0:T(8,128)S(1)}, f32[136,128]{1,0:T(8,128)S(1)}, u32[]{:S(2)}, u32[]{:S(2)}) collective-permute-start(f32[136,128]{1,0:T(8,128)S(1)} %get-tuple-element.31), channel_id=1, source_target_pairs={{0,8},{16,24},{8,0},{24,16},{1,9},{17,25},{9,1},{25,17},{2,10},{18... | collective-permute-start | bytes 208904 | tf_op jit(solution)/shard_map/ppermute | solution.py:466
